TPU v7x, 32 devices: a whole 2x2x4 slice. The times are simulated.
32 devices in a mesh: fsdp: 8 (over z, y), ctx: 4 (over x, core).
Axes of the slice: x: 2, y: 2, z: 4, core: 2. Of those that a mesh axis runs over, the one named last changes fastest.
Arguments:
- tokens: bfloat16 [2, 8, 256, 512], P(None, 'fsdp', 'ctx'), may hold values from -6 to 6
- cotangent: bfloat16 [2, 8, 256, 512], P(None, 'fsdp', 'ctx'), may hold values from -6 to 6
- doc_lengths: int32 [2, 8, 5], P(None, 'fsdp'), may hold values from 0 to 256, as said below
- w_qkv: bfloat16 [2, 512, 1536], P(None, ('fsdp', 'ctx')), may hold values from -0.25 to 0.25
- w_out: bfloat16 [2, 512, 512], P(None, ('fsdp', 'ctx')), may hold values from -1 to 1
- w_up: bfloat16 [2, 512, 2048], P(None, ('fsdp', 'ctx')), may hold values from -0.25 to 0.25
- w_down: bfloat16 [2, 2048, 512], P(None, ('fsdp', 'ctx')), may hold values from -0.125 to 0.125
- norm_gain: bfloat16 [2, 2, 512], P(None, None, ('fsdp', 'ctx')), may hold values from 0.25 to 1.75
- norm_bias: bfloat16 [2, 2, 512], P(None, None, ('fsdp', 'ctx')), may hold values from -1 to 1
- proj_bias: bfloat16 [2, 4608], P(None, ('fsdp', 'ctx')), may hold values from -1 to 1
Outputs:
- block_out: bfloat16 [2, 8, 256, 512], P(None, 'fsdp', 'ctx')
- grad_tokens: float32 [2, 8, 256, 512], P(None, 'fsdp', 'ctx')
- grad_w_qkv: float32 [2, 512, 1536], P(None, ('fsdp', 'ctx'))
- grad_w_out: float32 [2, 512, 512], P(None, ('fsdp', 'ctx'))
- grad_w_up: float32 [2, 512, 2048], P(None, ('fsdp', 'ctx'))
- grad_w_down: float32 [2, 2048, 512], P(None, ('fsdp', 'ctx'))
- grad_norm_gain: float32 [2, 2, 512], P(None, None, ('fsdp', 'ctx'))
- grad_norm_bias: float32 [2, 2, 512], P(None, None, ('fsdp', 'ctx'))
- grad_proj_bias: float32 [2, 4608], P(None, ('fsdp', 'ctx'))
Inputs may be any that keep to these rules, and one draw needn't show every extreme that they name: `doc_lengths`: each pack's 5 document lengths sum to 256; zero lengths occur. In micro-batch 0 the third document of every pack starts within its first 64 positions and ends within its last 64, and in one pack of micro-batch 0 it fills all 256 positions.
All inputs are finite; a program needn't handle non-finite values.
Results may differ from a plain program's by a relative error of at most 0.015.
Values may be sent and summed in bfloat16 or wider, within the bound.
A program may use at most 192 MiB of HBM per device.

v0:
```python
import jax
import jax.numpy as jnp
from jax import lax
from jax.sharding import PartitionSpec as P

HEAD = 64


masked_score = -1e30
norm_eps = 1e-05


def layer_norm(values, gain, shift):
    centred = values - jnp.mean(values, axis=-1, keepdims=True)
    spread = jnp.mean(centred * centred, axis=-1, keepdims=True)
    return centred * lax.rsqrt(spread + norm_eps) * gain + shift


def rotary_tables(positions):
    frequency = 10000.0 ** (-jnp.arange(8, dtype=jnp.float32) / 8.0)
    angles = positions.astype(jnp.float32)[:, None] * frequency[None, :]
    angles = jnp.concatenate([angles, angles], axis=1)
    return (jnp.cos(angles)[:, None, :], jnp.sin(angles)[:, None, :])


def rotate(heads_in, cos_table, sin_table):
    turned = heads_in[..., :16]
    swapped = jnp.concatenate([-turned[..., 8:], turned[..., :8]], axis=-1)
    return jnp.concatenate([turned * cos_table + swapped * sin_table, heads_in[..., 16:]], axis=-1)


def segments_of(lengths, positions):
    endings = jnp.cumsum(lengths)
    return jnp.sum((endings[None, :] <= positions[:, None]).astype(jnp.int32), axis=1)


def exact_gelu(inputs):
    return jax.nn.gelu(inputs, approximate=False)


def matmul(left, right):
    return jnp.dot(left, right, preferred_element_type=jnp.float32)


def matmul_tn(left, right):
    return lax.dot_general(
        left, right, (((0,), (0,)), ((), ())), preferred_element_type=jnp.float32
    )


def matmul_nt(left, right):
    return lax.dot_general(
        left, right, (((1,), (1,)), ((), ())), preferred_element_type=jnp.float32
    )


def forward_layer(values, weights, visible, cos_table, sin_table):
    w_qkv, w_out, w_up, w_down, gain_pair, shift_pair, biases = weights
    gain_pair = gain_pair.astype(jnp.float32)
    shift_pair = shift_pair.astype(jnp.float32)
    biases = biases.astype(jnp.float32)
    row_count, model_width = values.shape
    head_count = model_width // HEAD
    score_scale = HEAD ** (-0.5)
    normed = layer_norm(values, gain_pair[0], shift_pair[0]).astype(jnp.bfloat16)
    mixed_qkv = matmul(normed, w_qkv) + biases[: 3 * model_width]
    query_heads = rotate(
        mixed_qkv[:, :model_width].reshape(row_count, head_count, HEAD), cos_table, sin_table
    ).astype(jnp.bfloat16)
    key_own = rotate(
        mixed_qkv[:, model_width : 2 * model_width].reshape(row_count, head_count, HEAD),
        cos_table,
        sin_table,
    )
    key_own = key_own.astype(jnp.bfloat16).reshape(row_count, model_width)
    value_own = mixed_qkv[:, 2 * model_width :].astype(jnp.bfloat16)
    key_all, value_all = (
        lax.all_gather(key_own, "ctx", axis=0, tiled=True),
        lax.all_gather(value_own, "ctx", axis=0, tiled=True),
    )
    key_all = key_all.reshape(-1, head_count, HEAD)
    value_all = value_all.reshape(-1, head_count, HEAD)
    scores = (
        jnp.einsum("qhd,khd->hqk", query_heads, key_all, preferred_element_type=jnp.float32)
        * score_scale
    )
    scores = jnp.where(visible[None], scores, masked_score)
    row_peak = jnp.max(scores, axis=-1, keepdims=True)
    exp_scores = jnp.exp(scores - row_peak)
    row_total = jnp.sum(exp_scores, axis=-1, keepdims=True)
    soft_weights = exp_scores / row_total
    log_total = row_peak + jnp.log(row_total)
    attended = jnp.einsum(
        "hqk,khd->qhd",
        soft_weights.astype(jnp.bfloat16),
        value_all,
        preferred_element_type=jnp.float32,
    )
    attended = attended.reshape(row_count, model_width).astype(jnp.bfloat16)
    branch_attn = matmul(attended, w_out) + biases[3 * model_width : 4 * model_width]
    normed_mlp = layer_norm(values, gain_pair[1], shift_pair[1]).astype(jnp.bfloat16)
    upward = matmul(normed_mlp, w_up) + biases[5 * model_width :]
    activated = exact_gelu(upward).astype(jnp.bfloat16)
    branch_mlp = matmul(activated, w_down) + biases[4 * model_width : 5 * model_width]
    kept = (
        values,
        normed,
        query_heads,
        key_all,
        value_all,
        log_total,
        attended,
        normed_mlp,
        upward,
        activated,
    )
    return (values + branch_attn + branch_mlp, kept)


def backward_layer(upstream, weights, kept, visible, cos_table, sin_table):
    w_qkv, w_out, w_up, w_down, gain_pair, shift_pair, biases = weights
    gain_pair = gain_pair.astype(jnp.float32)
    shift_pair = shift_pair.astype(jnp.float32)
    (
        values,
        normed,
        query_heads,
        key_all,
        value_all,
        log_total,
        attended,
        normed_mlp,
        upward,
        activated,
    ) = kept
    row_count, model_width = values.shape
    head_count = model_width // HEAD
    score_scale = HEAD ** (-0.5)
    upstream_low = upstream.astype(jnp.bfloat16)
    grad_down = matmul_tn(activated, upstream_low)
    grad_out = matmul_tn(attended, upstream_low)
    branch_bias = jnp.sum(upstream_low.astype(jnp.float32), axis=0)
    grad_active = matmul_nt(upstream_low, w_down)
    gelu_value, gelu_pull = jax.vjp(exact_gelu, upward)
    grad_upward = gelu_pull(grad_active)[0].astype(jnp.bfloat16)
    grad_up = matmul_tn(normed_mlp, grad_upward)
    grad_normed_mlp = matmul_nt(grad_upward, w_up)
    second_value, second_pull = jax.vjp(layer_norm, values, gain_pair[1], shift_pair[1])
    grad_input_mlp, grad_gain_mlp, grad_shift_mlp = second_pull(grad_normed_mlp)
    grad_attended = (
        matmul_nt(upstream_low, w_out).astype(jnp.bfloat16).reshape(row_count, head_count, HEAD)
    )
    scores = (
        jnp.einsum("qhd,khd->hqk", query_heads, key_all, preferred_element_type=jnp.float32)
        * score_scale
    )
    scores = jnp.where(visible[None], scores, masked_score)
    soft_back = jnp.exp(scores - log_total)
    grad_soft = jnp.einsum(
        "qhd,khd->hqk", grad_attended, value_all, preferred_element_type=jnp.float32
    )
    grad_value_all = jnp.einsum(
        "hqk,qhd->khd",
        soft_back.astype(jnp.bfloat16),
        grad_attended,
        preferred_element_type=jnp.float32,
    )
    grad_value_all = grad_value_all.reshape(-1, model_width)
    row_inner = jnp.sum(soft_back * grad_soft, axis=-1, keepdims=True)
    grad_scores = (soft_back * (grad_soft - row_inner)).astype(jnp.bfloat16)
    grad_query = (
        jnp.einsum("hqk,khd->qhd", grad_scores, key_all, preferred_element_type=jnp.float32)
        * score_scale
    )
    grad_key_all = (
        jnp.einsum("hqk,qhd->khd", grad_scores, query_heads, preferred_element_type=jnp.float32)
        * score_scale
    )
    grad_key_all = grad_key_all.reshape(-1, model_width)
    grad_key, grad_value = (
        lax.psum_scatter(
            grad_key_all.astype(jnp.bfloat16), "ctx", scatter_dimension=0, tiled=True
        ).astype(jnp.float32),
        lax.psum_scatter(
            grad_value_all.astype(jnp.bfloat16), "ctx", scatter_dimension=0, tiled=True
        ).astype(jnp.float32),
    )
    grad_query = rotate(grad_query, cos_table, -sin_table).reshape(row_count, model_width)
    grad_key = rotate(grad_key.reshape(row_count, head_count, HEAD), cos_table, -sin_table).reshape(
        row_count, model_width
    )
    grad_mixed = jnp.concatenate([grad_query, grad_key, grad_value], axis=1).astype(jnp.bfloat16)
    grad_qkv = matmul_tn(normed, grad_mixed)
    grad_normed = matmul_nt(grad_mixed, w_qkv)
    first_value, first_pull = jax.vjp(layer_norm, values, gain_pair[0], shift_pair[0])
    grad_input_attn, grad_gain_attn, grad_shift_attn = first_pull(grad_normed)
    grad_biases = jnp.concatenate(
        [
            jnp.sum(grad_mixed.astype(jnp.float32), axis=0),
            branch_bias,
            branch_bias,
            jnp.sum(grad_upward.astype(jnp.float32), axis=0),
        ]
    )
    gradients = (
        grad_qkv,
        grad_out,
        grad_up,
        grad_down,
        jnp.stack([grad_gain_attn, grad_gain_mlp]),
        jnp.stack([grad_shift_attn, grad_shift_mlp]),
        grad_biases,
    )
    return (upstream + grad_input_attn + grad_input_mlp, gradients)


def body(
    tokens, cotangent, doc_lengths, w_qkv, w_out, w_up, w_down, norm_gain, norm_bias, proj_bias
):
    micro_count = tokens.shape[0]
    row_count = tokens.shape[2]
    layer_count = w_qkv.shape[0]
    ctx_place = lax.axis_index("ctx")
    pack_len = row_count * lax.axis_size("ctx")
    all_positions = jnp.arange(pack_len, dtype=jnp.int32)
    own_positions = ctx_place * row_count + jnp.arange(row_count, dtype=jnp.int32)
    cos_table, sin_table = rotary_tables(own_positions)
    totals = [None] * layer_count
    outputs = []
    input_grads = []
    for micro_index in range(micro_count):
        lengths = doc_lengths[micro_index, 0]
        seg_all = segments_of(lengths, all_positions)
        seg_own = segments_of(lengths, own_positions)
        visible = (all_positions[None, :] <= own_positions[:, None]) & (
            seg_all[None, :] == seg_own[:, None]
        )
        current = tokens[micro_index, 0].astype(jnp.float32)
        kept_layers = []
        for layer_index in range(layer_count):
            weights = (
                lax.all_gather(w_qkv[layer_index], ("fsdp", "ctx"), axis=0, tiled=True),
                lax.all_gather(w_out[layer_index], ("fsdp", "ctx"), axis=0, tiled=True),
                lax.all_gather(w_up[layer_index], ("fsdp", "ctx"), axis=0, tiled=True),
                lax.all_gather(w_down[layer_index], ("fsdp", "ctx"), axis=0, tiled=True),
                lax.all_gather(norm_gain[layer_index], ("fsdp", "ctx"), axis=1, tiled=True),
                lax.all_gather(norm_bias[layer_index], ("fsdp", "ctx"), axis=1, tiled=True),
                lax.all_gather(proj_bias[layer_index], ("fsdp", "ctx"), axis=0, tiled=True),
            )
            current, kept = forward_layer(current, weights, visible, cos_table, sin_table)
            kept_layers.append(kept)
        outputs.append(current.astype(jnp.bfloat16))
        upstream = cotangent[micro_index, 0].astype(jnp.float32)
        for layer_index in reversed(range(layer_count)):
            weights = (
                lax.all_gather(w_qkv[layer_index], ("fsdp", "ctx"), axis=0, tiled=True),
                lax.all_gather(w_out[layer_index], ("fsdp", "ctx"), axis=0, tiled=True),
                lax.all_gather(w_up[layer_index], ("fsdp", "ctx"), axis=0, tiled=True),
                lax.all_gather(w_down[layer_index], ("fsdp", "ctx"), axis=0, tiled=True),
                lax.all_gather(norm_gain[layer_index], ("fsdp", "ctx"), axis=1, tiled=True),
                lax.all_gather(norm_bias[layer_index], ("fsdp", "ctx"), axis=1, tiled=True),
                lax.all_gather(proj_bias[layer_index], ("fsdp", "ctx"), axis=0, tiled=True),
            )
            upstream, gradients = backward_layer(
                upstream, weights, kept_layers[layer_index], visible, cos_table, sin_table
            )
            if totals[layer_index] is None:
                totals[layer_index] = gradients
            else:
                totals[layer_index] = tuple(
                    (running + fresh for running, fresh in zip(totals[layer_index], gradients))
                )
        input_grads.append(upstream)
    summed_layers = []
    for layer_index in range(layer_count):
        layer_sums = totals[layer_index]
        summed_layers.append(
            (
                lax.psum_scatter(layer_sums[0], ("fsdp", "ctx"), scatter_dimension=0, tiled=True),
                lax.psum_scatter(layer_sums[1], ("fsdp", "ctx"), scatter_dimension=0, tiled=True),
                lax.psum_scatter(layer_sums[2], ("fsdp", "ctx"), scatter_dimension=0, tiled=True),
                lax.psum_scatter(layer_sums[3], ("fsdp", "ctx"), scatter_dimension=0, tiled=True),
                lax.psum_scatter(layer_sums[4], ("fsdp", "ctx"), scatter_dimension=1, tiled=True),
                lax.psum_scatter(layer_sums[5], ("fsdp", "ctx"), scatter_dimension=1, tiled=True),
                lax.psum_scatter(layer_sums[6], ("fsdp", "ctx"), scatter_dimension=0, tiled=True),
            )
        )
    totals = summed_layers
    results = [
        jnp.stack([totals[layer_index][member] for layer_index in range(layer_count)])
        for member in range(7)
    ]
    return (
        jnp.stack(outputs)[:, None],
        jnp.stack(input_grads)[:, None],
        results[0],
        results[1],
        results[2],
        results[3],
        results[4],
        results[5],
        results[6],
    )


def solution(mesh):
    placed = (
        P(None, "fsdp", "ctx", None),
        P(None, "fsdp", "ctx", None),
        P(None, "fsdp", None),
        P(None, ("fsdp", "ctx"), None),
        P(None, ("fsdp", "ctx"), None),
        P(None, ("fsdp", "ctx"), None),
        P(None, ("fsdp", "ctx"), None),
        P(None, None, ("fsdp", "ctx")),
        P(None, None, ("fsdp", "ctx")),
        P(None, ("fsdp", "ctx")),
    )
    return jax.shard_map(
        body,
        mesh=mesh,
        in_specs=placed,
        out_specs=(
            P(None, "fsdp", "ctx", None),
            P(None, "fsdp", "ctx", None),
            P(None, ("fsdp", "ctx"), None),
            P(None, ("fsdp", "ctx"), None),
            P(None, ("fsdp", "ctx"), None),
            P(None, ("fsdp", "ctx"), None),
            P(None, None, ("fsdp", "ctx")),
            P(None, None, ("fsdp", "ctx")),
            P(None, ("fsdp", "ctx")),
        ),
        check_vma=False,
    )
```

profile of v0, /device:TPU:6, one launch (start us, length us, event | category | flops | bytes accessed | tf_op | source)
XLA Modules:
  0.0 2150.4 jit_solution(14744593420776543412)
XLA Ops:
  15.2 40.7 %all-reduce.5 = (bf16[4608]{0:T(1024)(128)(2,1)S(1)}, bf16[4608]{0:T(1024)(128)(2,1)S(1)}) all-reduce(bf16[4608]{0:T(1024)(128)(2,1)S(1)} %dynamic-update-slice, bf16[4608]{0:T(1024)(128)(2,1)S(1)} %dynamic-update-slice.1), channel_id=5, replica_groups=mesh['fsdp'=8,'ctx'=4] {'fsdp','ctx'}, use_global_device_ids=true, to_apply=%add | all-reduce | flops 9216 | bytes 36864
  59.1 34.8 %all-gather.11 = bf16[1,512,512]{2,1,0:T(8,128)(2,1)S(1)} all-gather(bf16[1,16,512]{2,1,0:T(8,128)(2,1)S(1)} %get-tuple-element.190), channel_id=13, replica_groups=mesh['fsdp'=8,'ctx'=4] {'fsdp','ctx'}, dimensions={1}, use_global_device_ids=true | all-gather | bytes 540672 | tf_op jit(solution)/shard_map/all_gather | solution.py:243
  98.1 41.3 %all-gather = bf16[1,2,512]{1,0,2:T(2,128)(2,1)S(1)} all-gather(bf16[1,2,16]{1,0,2:T(2,128)(2,1)S(1)} %copy.550), channel_id=2, replica_groups=mesh['fsdp'=8,'ctx'=4] {'fsdp','ctx'}, dimensions={2}, use_global_device_ids=true | all-gather | bytes 2112 | tf_op jit(solution)/shard_map/all_gather | solution.py:246
  139.7 2.7 slice_reduce_fusion.5
  142.4 37.4 %all-gather.1 = bf16[1,2,512]{1,0,2:T(2,128)(2,1)S(1)} all-gather(bf16[1,2,16]{1,0,2:T(2,128)(2,1)S(1)} %copy.551), channel_id=3, replica_groups=mesh['fsdp'=8,'ctx'=4] {'fsdp','ctx'}, dimensions={2}, use_global_device_ids=true | all-gather | bytes 2112 | tf_op jit(solution)/shard_map/all_gather | solution.py:247
  180.2 3.3 slice_reduce_fusion.4
  183.5 38.9 %all-gather.7 = bf16[1,2,512]{1,0,2:T(2,128)(2,1)S(1)} all-gather(bf16[1,2,16]{1,0,2:T(2,128)(2,1)S(1)} %copy.552), channel_id=9, replica_groups=mesh['fsdp'=8,'ctx'=4] {'fsdp','ctx'}, dimensions={2}, use_global_device_ids=true | all-gather | bytes 2112 | tf_op jit(solution)/shard_map/all_gather | solution.py:246
  222.7 3.4 slice_reduce_fusion.1
  226.0 37.7 %all-gather.8 = bf16[1,2,512]{1,0,2:T(2,128)(2,1)S(1)} all-gather(bf16[1,2,16]{1,0,2:T(2,128)(2,1)S(1)} %copy.553), channel_id=10, replica_groups=mesh['fsdp'=8,'ctx'=4] {'fsdp','ctx'}, dimensions={2}, use_global_device_ids=true | all-gather | bytes 2112 | tf_op jit(solution)/shard_map/all_gather | solution.py:247
  264.0 3.3 slice_reduce_fusion
  268.2 39.8 %all-gather.4 = bf16[1,512,512]{2,1,0:T(8,128)(2,1)S(1)} all-gather(bf16[1,16,512]{2,1,0:T(8,128)(2,1)S(1)} %get-tuple-element.191), channel_id=6, replica_groups=mesh['fsdp'=8,'ctx'=4] {'fsdp','ctx'}, dimensions={1}, use_global_device_ids=true | all-gather | bytes 540672 | tf_op jit(solution)/shard_map/all_gather | solution.py:243
  318.0 5.8 all_gather.118
  324.7 5.8 all_gather.48
  330.9 5.9 all_gather.49
  339.0 3.9 multiply_convert_fusion.7
  349.7 6.0 all_gather.113
  360.7 5.9 all_gather.114
  366.7 6.3 all_gather.119
  386.1 5.9 all_gather.120
  394.6 5.9 all_gather.121
  423.2 3.1 convolution_add_fusion.12
  428.3 4.0 convert_reduce_fusion.1
  440.6 4.2 reduce-scatter.37.cloned.1.call-done
  458.2 9.7 reduce-scatter.31.cloned.1.call-done
  470.0 20.4 reduce-scatter.39.cloned.1.call-done
  522.5 3.9 convert_reduce_fusion.2
  526.5 2.8 convert_reduce_fusion.3
  534.0 10.1 reduce-scatter.33.cloned.1.call-done
  571.7 18.0 reduce-scatter.35.cloned.1.call-done
  608.4 2.6 fusion.226
  611.0 3.8 convolution_add_fusion.2
  616.5 3.9 convolution_add_fusion.3
  622.2 2.8 convolution_add_fusion.4
  626.8 2.7 convolution_add_fusion.5
  630.9 3.2 fusion.86
  636.4 75.0 %reduce-scatter.67.cloned.1.call-done = f32[16,2]{1,0:T(8,128)} async-done(((f32[512,2]{1,0:T(8,128)}), f32[16,2]{1,0:T(8,128)}) %reduce-scatter.67.cloned.1.call-update) | async-done | bytes 144
  712.2 130.8 %reduce-scatter.63.cloned.1.call-done = f32[16,2]{1,0:T(8,128)} async-done(((f32[512,2]{1,0:T(8,128)}), f32[16,2]{1,0:T(8,128)}) %reduce-scatter.63.cloned.1.call-update) | async-done | bytes 144
  844.3 51.9 %all-reduce.4 = (f32[4608]{0:T(1024)S(1)}, f32[4608]{0:T(1024)S(1)}) all-reduce(f32[4608]{0:T(1024)S(1)} %maximum_add_fusion.1, f32[4608]{0:T(1024)S(1)} %maximum_add_fusion), channel_id=37, replica_groups=mesh['fsdp'=8,'ctx'=4] {'fsdp','ctx'}, use_global_device_ids=true, to_apply=%region_91.92.clone | all-reduce | flops 9216 | bytes 73728
  897.9 77.2 %reduce-scatter.61.cloned.1.call-done = f32[16,2]{1,0:T(8,128)} async-done(((f32[512,2]{1,0:T(8,128)}), f32[16,2]{1,0:T(8,128)}) %reduce-scatter.61.cloned.1.call-update) | async-done | bytes 144
  975.9 131.3 %reduce-scatter.65.cloned.1.call-done = f32[16,2]{1,0:T(8,128)} async-done(((f32[512,2]{1,0:T(8,128)}), f32[16,2]{1,0:T(8,128)}) %reduce-scatter.65.cloned.1.call-update) | async-done | bytes 144
  1109.1 131.1 %reduce-scatter.51.cloned.1.call-done = f32[16,512]{1,0:T(8,128)} async-done(((f32[512,512]{1,0:T(8,128)}), f32[16,512]{1,0:T(8,128)}) %reduce-scatter.51.cloned.1.call-update) | async-done | bytes 32784 | tf_op jit(solution)/shard_map/reduce_scatter | solution.py:280
  1240.2 133.0 %reduce-scatter.49.cloned.1.call-done = f32[16,512]{1,0:T(8,128)} async-done(((f32[512,512]{1,0:T(8,128)}), f32[16,512]{1,0:T(8,128)}) %reduce-scatter.49.cloned.1.call-update) | async-done | bytes 32784 | tf_op jit(solution)/shard_map/reduce_scatter | solution.py:280
  1374.6 116.4 %reduce-scatter.47.cloned.1.call-done = f32[16,1536]{1,0:T(8,128)} async-done(((f32[512,1536]{1,0:T(8,128)}), f32[16,1536]{1,0:T(8,128)}) %reduce-scatter.47.cloned.1.call-update) | async-done | bytes 98320 | tf_op jit(solution)/shard_map/reduce_scatter | solution.py:279
  1491.0 106.0 %reduce-scatter.45.cloned.1.call-done = f32[16,1536]{1,0:T(8,128)} async-done(((f32[512,1536]{1,0:T(8,128)}), f32[16,1536]{1,0:T(8,128)}) %reduce-scatter.45.cloned.1.call-update) | async-done | bytes 98320 | tf_op jit(solution)/shard_map/reduce_scatter | solution.py:279
  1598.5 125.9 %reduce-scatter.59.cloned.1.call-done = f32[64,512]{1,0:T(8,128)} async-done(((f32[2048,512]{1,0:T(8,128)}), f32[64,512]{1,0:T(8,128)}) %reduce-scatter.59.cloned.1.call-update) | async-done | bytes 131088 | tf_op jit(solution)/shard_map/reduce_scatter | solution.py:282
  1724.5 139.0 %reduce-scatter.57.cloned.1.call-done = f32[64,512]{1,0:T(8,128)} async-done(((f32[2048,512]{1,0:T(8,128)}), f32[64,512]{1,0:T(8,128)}) %reduce-scatter.57.cloned.1.call-update) | async-done | bytes 131088 | tf_op jit(solution)/shard_map/reduce_scatter | solution.py:282
  1865.1 137.5 %reduce-scatter.55.cloned.1.call-done = f32[16,2048]{1,0:T(8,128)} async-done(((f32[512,2048]{1,0:T(8,128)}), f32[16,2048]{1,0:T(8,128)}) %reduce-scatter.55.cloned.1.call-update) | async-done | bytes 131088 | tf_op jit(solution)/shard_map/reduce_scatter | solution.py:281
  2002.7 139.1 %reduce-scatter.53.cloned.1.call-done = f32[16,2048]{1,0:T(8,128)} async-done(((f32[512,2048]{1,0:T(8,128)}), f32[16,2048]{1,0:T(8,128)}) %reduce-scatter.53.cloned.1.call-update) | async-done | bytes 131088 | tf_op jit(solution)/shard_map/reduce_scatter | solution.py:281
  (793 shorter events, 208.1 us)
Async XLA Ops:
  7.2 301.6 %all-gather.21.cloned.1.call-start = ((), (), s32[]{:S(2)}) async-start(), calls=%async_computation.36 | async-start | bytes 1622016 | tf_op jit(solution)/shard_map/all_gather | solution.py:242
  8.8 330.1 %all-gather.23.cloned.1.call-start = ((), (), s32[]{:S(2)}) async-start(), calls=%async_computation.37 | async-start | bytes 2162688 | tf_op jit(solution)/shard_map/all_gather | solution.py:244
  10.4 332.5 %all-gather.25.cloned.1.call-start = ((), (), s32[]{:S(2)}) async-start(), calls=%async_computation.38 | async-start | bytes 2162688 | tf_op jit(solution)/shard_map/all_gather | solution.py:245
  12.0 333.4 %all-gather.27.cloned.1.call-start = ((), (), s32[]{:S(2)}) async-start(), calls=%async_computation.39 | async-start | bytes 1622016 | tf_op jit(solution)/shard_map/all_gather | solution.py:242
  12.6 410.6 %all-gather.29.cloned.1.call-start = ((), (), s32[]{:S(2)}) async-start(), calls=%async_computation.40 | async-start | bytes 2162688 | tf_op jit(solution)/shard_map/all_gather | solution.py:244
  13.2 415.1 %all-gather.31.cloned.1.call-start = ((), (), s32[]{:S(2)}) async-start(), calls=%async_computation.41 | async-start | bytes 2162688 | tf_op jit(solution)/shard_map/all_gather | solution.py:245
  13.8 424.9 %reduce-scatter.29.cloned.1.call-start = ((), (), s32[]{:S(2)}) async-start(), calls=%async_computation.20 | async-start | bytes 327680 | tf_op jit(solution)/shard_map/reduce_scatter | solution.py:181
  56.5 252.3 %copy-start.127 = (f32[1536]{0:T(1024)}, f32[1536]{0:T(1024)S(1)}, u32[]{:S(2)}) copy-start(f32[1536]{0:T(1024)S(1)} %slice_reduce_fusion.9) | copy-start | bytes 18436
  96.2 212.7 %copy-start.136 = (f32[64]{0:T(128)}, f32[64]{0:T(128)S(1)}, u32[]{:S(2)}) copy-start(f32[64]{0:T(128)S(1)} %broadcast_multiply_fusion.2) | copy-start | bytes 772
  97.0 211.9 %copy-start.156 = (f32[64]{0:T(128)}, f32[64]{0:T(128)S(1)}, u32[]{:S(2)}) copy-start(f32[64]{0:T(128)S(1)} %fusion.247) | copy-start | bytes 772
  401.9 42.9 %reduce-scatter.37.cloned.1.call-start = ((), (), s32[]{:S(2)}) async-start(), calls=%async_computation.24 | async-start | bytes 327680 | tf_op jit(solution)/shard_map/reduce_scatter | solution.py:181
  410.3 57.6 %reduce-scatter.31.cloned.1.call-start = ((), (), s32[]{:S(2)}) async-start(), calls=%async_computation.21 | async-start | bytes 327680 | tf_op jit(solution)/shard_map/reduce_scatter | solution.py:184
  414.5 76.0 %reduce-scatter.39.cloned.1.call-start = ((), (), s32[]{:S(2)}) async-start(), calls=%async_computation.25 | async-start | bytes 327680 | tf_op jit(solution)/shard_map/reduce_scatter | solution.py:184
  423.0 107.8 %reduce-scatter.41.cloned.1.call-start = ((), (), s32[]{:S(2)}) async-start(), calls=%async_computation.26 | async-start | bytes 327680 | tf_op jit(solution)/shard_map/reduce_scatter | solution.py:181
  501.3 42.7 %reduce-scatter.33.cloned.1.call-start = ((), (), s32[]{:S(2)}) async-start(), calls=%async_computation.22 | async-start | bytes 327680 | tf_op jit(solution)/shard_map/reduce_scatter | solution.py:181
  505.8 63.7 %reduce-scatter.43.cloned.1.call-start = ((), (), s32[]{:S(2)}) async-start(), calls=%async_computation.27 | async-start | bytes 327680 | tf_op jit(solution)/shard_map/reduce_scatter | solution.py:184
  512.7 77.0 %reduce-scatter.35.cloned.1.call-start = ((), (), s32[]{:S(2)}) async-start(), calls=%async_computation.23 | async-start | bytes 327680 | tf_op jit(solution)/shard_map/reduce_scatter | solution.py:184
  516.7 194.7 %reduce-scatter.67.cloned.1.call-start = ((), (), s32[]{:S(2)}) async-start(), calls=%async_computation.45 | async-start | bytes 270336
  519.2 323.8 %reduce-scatter.63.cloned.1.call-start = ((), (), s32[]{:S(2)}) async-start(), calls=%async_computation.43 | async-start | bytes 270336
  522.2 452.9 %reduce-scatter.61.cloned.1.call-start = ((), (), s32[]{:S(2)}) async-start(), calls=%async_computation.42 | async-start | bytes 270336
  596.8 510.4 %reduce-scatter.65.cloned.1.call-start = ((), (), s32[]{:S(2)}) async-start(), calls=%async_computation.44 | async-start | bytes 270336
  597.8 642.4 %reduce-scatter.51.cloned.1.call-start = ((), (), s32[]{:S(2)}) async-start(), calls=%async_computation.31 | async-start | bytes 1081344 | tf_op jit(solution)/shard_map/reduce_scatter | solution.py:280
  599.2 774.0 %reduce-scatter.49.cloned.1.call-start = ((), (), s32[]{:S(2)}) async-start(), calls=%async_computation.30 | async-start | bytes 1081344 | tf_op jit(solution)/shard_map/reduce_scatter | solution.py:280
  600.8 890.1 %reduce-scatter.47.cloned.1.call-start = ((), (), s32[]{:S(2)}) async-start(), calls=%async_computation.29 | async-start | bytes 3244032 | tf_op jit(solution)/shard_map/reduce_scatter | solution.py:279
  604.1 992.8 %reduce-scatter.45.cloned.1.call-start = ((), (), s32[]{:S(2)}) async-start(), calls=%async_computation.28 | async-start | bytes 3244032 | tf_op jit(solution)/shard_map/reduce_scatter | solution.py:279
  608.1 1116.4 %reduce-scatter.59.cloned.1.call-start = ((), (), s32[]{:S(2)}) async-start(), calls=%async_computation.35 | async-start | bytes 4325376 | tf_op jit(solution)/shard_map/reduce_scatter | solution.py:282
  614.9 1248.6 %reduce-scatter.57.cloned.1.call-start = ((), (), s32[]{:S(2)}) async-start(), calls=%async_computation.34 | async-start | bytes 4325376 | tf_op jit(solution)/shard_map/reduce_scatter | solution.py:282
  620.4 1382.2 %reduce-scatter.55.cloned.1.call-start = ((), (), s32[]{:S(2)}) async-start(), calls=%async_computation.33 | async-start | bytes 4325376 | tf_op jit(solution)/shard_map/reduce_scatter | solution.py:281
  625.0 1516.7 %reduce-scatter.53.cloned.1.call-start = ((), (), s32[]{:S(2)}) async-start(), calls=%async_computation.32 | async-start | bytes 4325376 | tf_op jit(solution)/shard_map/reduce_scatter | solution.py:281
  634.2 209.8 %copy-start.34 = (f32[64,512]{1,0:T(8,128)S(1)}, f32[64,512]{1,0:T(8,128)}, u32[]{:S(2)}) copy-start(f32[64,512]{1,0:T(8,128)} %fusion.22) | copy-start | bytes 393220
  634.2 209.8 %copy-start.37 = (f32[64,512]{1,0:T(8,128)S(1)}, f32[64,512]{1,0:T(8,128)}, u32[]{:S(2)}) copy-start(f32[64,512]{1,0:T(8,128)} %fusion.34) | copy-start | bytes 393220
  634.2 209.8 %copy-start.47 = (f32[64,512]{1,0:T(8,128)S(1)}, f32[64,512]{1,0:T(8,128)}, u32[]{:S(2)}) copy-start(f32[64,512]{1,0:T(8,128)} %copy-done.46) | copy-start | bytes 393220
  634.2 209.8 %copy-start.49 = (f32[64,512]{1,0:T(8,128)S(1)}, f32[64,512]{1,0:T(8,128)}, u32[]{:S(2)}) copy-start(f32[64,512]{1,0:T(8,128)} %copy-done.48) | copy-start | bytes 393220
  634.2 209.8 %copy-start.183 = (f32[64]{0:T(128)S(1)}, f32[64]{0:T(128)}, u32[]{:S(2)}) copy-start(f32[64]{0:T(128)} %copy-done.182) | copy-start | bytes 772
  634.2 209.8 %copy-start.195 = (f32[64]{0:T(128)S(1)}, f32[64]{0:T(128)}, u32[]{:S(2)}) copy-start(f32[64]{0:T(128)} %copy-done.194) | copy-start | bytes 772
  634.2 209.8 %copy-start.197 = (f32[64]{0:T(128)S(1)}, f32[64]{0:T(128)}, u32[]{:S(2)}) copy-start(f32[64]{0:T(128)} %copy-done.196) | copy-start | bytes 772
  634.2 209.8 %copy-start.199 = (f32[64]{0:T(128)S(1)}, f32[64]{0:T(128)}, u32[]{:S(2)}) copy-start(f32[64]{0:T(128)} %copy-done.198) | copy-start | bytes 772
  634.2 210.0 %copy-start.176 = (f32[2048]{0:T(1024)S(1)}, f32[2048]{0:T(1024)}, u32[]{:S(2)}) copy-start(f32[2048]{0:T(1024)} %get-tuple-element.258) | copy-start | bytes 24580
  634.3 210.0 %copy-start.177 = (f32[2048]{0:T(1024)S(1)}, f32[2048]{0:T(1024)}, u32[]{:S(2)}) copy-start(f32[2048]{0:T(1024)} %get-tuple-element.260) | copy-start | bytes 24580
  635.5 261.4 %copy-start.205 = (f32[64]{0:T(128)S(1)}, f32[64]{0:T(128)}, u32[]{:S(2)}) copy-start(f32[64]{0:T(128)} %get-tuple-element.97) | copy-start | bytes 772
  635.5 261.4 %copy-start.203 = (f32[64]{0:T(128)S(1)}, f32[64]{0:T(128)}, u32[]{:S(2)}) copy-start(f32[64]{0:T(128)} %get-tuple-element.70) | copy-start | bytes 772
  635.5 261.4 %copy-start.39 = (f32[64,512]{1,0:T(8,128)S(1)}, f32[64,512]{1,0:T(8,128)}, u32[]{:S(2)}) copy-start(f32[64,512]{1,0:T(8,128)} %copy-done.38) | copy-start | bytes 393220
  635.5 261.4 %copy-start.43 = (f32[64,512]{1,0:T(8,128)S(1)}, f32[64,512]{1,0:T(8,128)}, u32[]{:S(2)}) copy-start(f32[64,512]{1,0:T(8,128)} %copy-done.42) | copy-start | bytes 393220
  635.6 261.4 %copy-start.45 = (f32[64,512]{1,0:T(8,128)S(1)}, f32[64,512]{1,0:T(8,128)}, u32[]{:S(2)}) copy-start(f32[64,512]{1,0:T(8,128)} %copy-done.44) | copy-start | bytes 393220
  635.6 261.4 %copy-start.181 = (f32[64]{0:T(128)S(1)}, f32[64]{0:T(128)}, u32[]{:S(2)}) copy-start(f32[64]{0:T(128)} %copy-done.180) | copy-start | bytes 772
  635.6 261.4 %copy-start.185 = (f32[64]{0:T(128)S(1)}, f32[64]{0:T(128)}, u32[]{:S(2)}) copy-start(f32[64]{0:T(128)} %copy-done.184) | copy-start | bytes 772
  635.6 261.4 %copy-start.187 = (f32[64]{0:T(128)S(1)}, f32[64]{0:T(128)}, u32[]{:S(2)}) copy-start(f32[64]{0:T(128)} %copy-done.186) | copy-start | bytes 772
  635.6 261.4 %copy-start.189 = (f32[64]{0:T(128)S(1)}, f32[64]{0:T(128)}, u32[]{:S(2)}) copy-start(f32[64]{0:T(128)} %copy-done.188) | copy-start | bytes 772
  (188 other events, 2834.6 us)
Sparse Core Ops, SparseCore 0:
  11.5 55.1 all-gather.20
  70.1 55.6 all-gather.22
  129.3 55.6 all-gather.24
  187.7 54.2 all-gather.26
  244.7 56.5 all-gather.28
  304.0 55.3 all-gather.30
  402.0 19.9 reduce-scatter.28
  424.6 20.1 reduce-scatter.36
  447.8 20.0 reduce-scatter.30
  470.4 20.0 reduce-scatter.38
  501.4 20.0 reduce-scatter.40
  524.0 20.0 reduce-scatter.32
  547.1 20.0 reduce-scatter.42
  569.6 20.0 reduce-scatter.34
  591.8 119.5 reduce-scatter.66
  713.6 129.3 reduce-scatter.62
  845.7 129.3 reduce-scatter.60
  977.8 129.3 reduce-scatter.64
  1109.4 130.7 reduce-scatter.50
  1242.4 130.7 reduce-scatter.48
  1378.6 112.3 reduce-scatter.46
  1496.4 100.4 reduce-scatter.44
  1599.2 125.2 reduce-scatter.58
  1726.6 136.7 reduce-scatter.56
  1865.7 136.9 reduce-scatter.54
  2004.8 136.8 reduce-scatter.52
where the time goes:
time: 2180 us; the launch traced here: 2150 us
  waiting for transfers between devices  1510 us (69%)
  blocking collectives  370 us (17%)
  matrix products  108 us (5%)
  local copies, waits for them, and re-layouts  93 us (4%)
  other arithmetic  52.8 us (2%)
    unnamed x30, waiting for transfers between devices  416 us
    reduce_scatter x2, waiting for transfers between devices, body(): lax.psum_scatter(layer_sums[2], ('fsdp', 'ctx'), scatter_dimension=0, til...  277 us
    reduce_scatter x2, waiting for transfers between devices, body(): lax.psum_scatter(layer_sums[3], ('fsdp', 'ctx'), scatter_dimension=0, til...  265 us
    reduce_scatter x2, waiting for transfers between devices, body(): lax.psum_scatter(layer_sums[1], ('fsdp', 'ctx'), scatter_dimension=0, til...  264 us
    reduce_scatter x2, waiting for transfers between devices, body(): lax.psum_scatter(layer_sums[0], ('fsdp', 'ctx'), scatter_dimension=0, til...  222 us
    unnamed x2, blocking collectives  92.7 us
    all_gather x2, blocking collectives, body(): lax.all_gather(norm_gain[layer_index], ('fsdp', 'ctx'), axis=1, tiled=True)  80.3 us
    all_gather x2, blocking collectives, body(): lax.all_gather(norm_bias[layer_index], ('fsdp', 'ctx'), axis=1, tiled=True)  75.2 us
  transfers between devices with their start and end apart: 26, of which 17 were waited for; matrix products, arithmetic and copies ran while one was open for 11% of the time, Pallas kernels for 0%

commit v1 on v0

v1 whole, which is shorter than its diff:
```python
import jax
import jax.numpy as jnp
from jax import lax
from jax.sharding import PartitionSpec as P

HEAD = 64
LANES = 128

masked_score = -1e30
norm_eps = 1e-05
low = jnp.bfloat16
wide = jnp.float32


def matmul(left, right):
    return jnp.dot(left, right, preferred_element_type=wide)


def matmul_tn(left, right):
    return lax.dot_general(left, right, (((0,), (0,)), ((), ())), preferred_element_type=wide)


def matmul_nt(left, right):
    return lax.dot_general(left, right, (((1,), (1,)), ((), ())), preferred_element_type=wide)


def normalise(values):
    centred = values - jnp.mean(values, axis=-1, keepdims=True)
    inverse = lax.rsqrt(jnp.mean(centred * centred, axis=-1, keepdims=True) + norm_eps)
    return centred * inverse, inverse


def rotary_tables(positions):
    frequency = 10000.0 ** (-jnp.arange(8, dtype=wide) / 8.0)
    angles = positions.astype(wide)[:, None] * frequency[None, :]
    angles = jnp.concatenate([angles, angles], axis=1)
    return jnp.cos(angles)[:, None, :], jnp.sin(angles)[:, None, :]


def rotate(heads_in, cos_table, sin_table):
    turned = heads_in[..., :16]
    swapped = jnp.concatenate([-turned[..., 8:], turned[..., :8]], axis=-1)
    return jnp.concatenate([turned * cos_table + swapped * sin_table, heads_in[..., 16:]], axis=-1)


def segments_of(lengths, positions):
    endings = jnp.cumsum(lengths, axis=-1)
    return jnp.sum((endings[:, None, :] <= positions[None, :, None]).astype(jnp.int32), axis=-1)


def slabs(array):
    pieces = array.shape[-1] // LANES
    return [array[..., LANES * i : LANES * (i + 1)] for i in range(pieces)]


def body(
    tokens, cotangent, doc_lengths, w_qkv, w_out, w_up, w_down, norm_gain, norm_bias, proj_bias
):
    micros, _, rows, width = tokens.shape
    layers = w_qkv.shape[0]
    C = lax.axis_size("ctx")
    F = lax.axis_size("fsdp")
    place = lax.axis_index("ctx")
    hidden = w_down.shape[1]
    depth = w_qkv.shape[1]
    local_qk = width // C
    heads = local_qk // HEAD
    local_ff = F * hidden
    pack_len = rows * C
    total_rows = C * micros * rows
    score_scale = HEAD ** (-0.5)
    own_bias = proj_bias.shape[1]
    own_small = own_bias + 4 * depth
    small_pad = -(-own_small // LANES) * LANES
    out_rows = local_qk // F

    forth = [(b, (b % F) * C + b // F) for b in range(F * C)]
    back = [(there, here) for here, there in forth]

    small_own = jnp.concatenate(
        [proj_bias, norm_gain.reshape(layers, -1), norm_bias.reshape(layers, -1)], axis=1
    )
    small_own = jnp.pad(small_own, ((0, 0), (0, small_pad - own_small)))
    qkv_cols = w_qkv.reshape(layers, depth, 3, C, local_qk).transpose(3, 0, 2, 1, 4)
    up_cols = w_up.reshape(layers, depth, F, C, hidden).transpose(3, 0, 1, 2, 4)
    up_cols = up_cols.reshape(C, layers, depth, local_ff // LANES, LANES).transpose(0, 1, 3, 2, 4)
    spread = jnp.concatenate(
        [
            qkv_cols.reshape(C, layers, -1, LANES),
            up_cols.reshape(C, layers, -1, LANES),
            jnp.broadcast_to(
                small_own.reshape(1, layers, -1, LANES), (C, layers, small_pad // LANES, LANES)
            ),
        ],
        axis=2,
    )
    arrived = lax.all_to_all(spread, "ctx", 0, 0, tiled=False)
    w_out_here = lax.ppermute(w_out, ("fsdp", "ctx"), forth)
    n_qkv = 3 * depth
    n_up = local_ff // LANES * depth
    column_slabs = 3 + local_ff // LANES

    tokens_rows = tokens.reshape(micros * rows, width)
    cot_rows = cotangent.reshape(micros * rows, width)
    both = lax.all_gather(jnp.stack([tokens_rows, cot_rows]), "ctx", axis=0)
    values_all = both[:, 0].reshape(total_rows, width).astype(wide)
    cot_all = both[:, 1].reshape(total_rows, width)

    def layer_weights(layer):
        part = arrived[:, layer]
        down_slabs = jnp.concatenate(slabs(w_down[layer]), axis=0)
        out_slabs = jnp.concatenate(slabs(w_out_here[layer]), axis=0)
        payload = jnp.concatenate(
            [part.reshape(-1, LANES), down_slabs, out_slabs], axis=0
        )
        size = payload.shape[0]
        if layer == 0:
            gathered = lax.all_to_all(
                jnp.broadcast_to(payload[None], (F, size, LANES)), "fsdp", 0, 0, tiled=False
            )
        else:
            gathered = lax.all_gather(payload, "fsdp", axis=0)
        n_part = part.size // LANES
        columns = gathered[:, :n_part].reshape(F, C, -1, LANES)
        qkv = columns[:, :, :n_qkv].reshape(F, C, 3, depth, LANES)
        qkv = [qkv[:, :, i].reshape(width, LANES) for i in range(3)]
        up = columns[:, :, n_qkv : n_qkv + n_up].reshape(F, C, -1, depth, LANES)
        up = [up[:, :, i].reshape(width, LANES) for i in range(local_ff // LANES)]
        small = columns[:, :, n_qkv + n_up :].reshape(F, C, small_pad).astype(wide)
        down = gathered[:, n_part : n_part + down_slabs.shape[0]].reshape(F, -1, hidden, LANES)
        down = [down[:, i].reshape(local_ff, LANES) for i in range(width // LANES)]
        out = gathered[:, n_part + down_slabs.shape[0] :].reshape(F, -1, out_rows, LANES)
        out = [out[:, i].reshape(local_qk, LANES) for i in range(width // LANES)]
        biases = small[:, :, :own_bias].reshape(-1)
        gains = small[:, :, own_bias : own_bias + 2 * depth].reshape(F * C, 2, depth)
        gains = gains.transpose(1, 0, 2).reshape(2, width)
        shifts = small[:, :, own_bias + 2 * depth : own_small].reshape(F * C, 2, depth)
        shifts = shifts.transpose(1, 0, 2).reshape(2, width)
        b_qkv = biases[: 3 * width].reshape(3, C, local_qk)
        b_qkv = lax.dynamic_slice_in_dim(b_qkv, place, 1, 1).reshape(-1)
        b_up = biases[5 * width :].reshape(F, C, hidden)
        b_up = lax.dynamic_slice_in_dim(b_up, place, 1, 1).reshape(-1)
        b_rest = biases[3 * width : 4 * width] + biases[4 * width : 5 * width]
        return (
            jnp.concatenate(qkv, axis=1),
            jnp.concatenate(out, axis=1),
            jnp.concatenate(up, axis=1),
            jnp.concatenate(down, axis=1),
            gains,
            shifts,
            b_qkv,
            b_up,
            b_rest,
        )

    def sum_rows(partial):
        parts = partial.astype(low).reshape(C, micros * rows, width)
        parts = lax.all_to_all(parts, "ctx", 0, 0, tiled=False)
        return jnp.sum(parts.astype(wide), axis=0)

    def gather_rows(own):
        return lax.all_gather(own, "ctx", axis=0).reshape(total_rows, width)

    positions = jnp.arange(pack_len, dtype=jnp.int32)
    seg = segments_of(doc_lengths[:, 0], positions)
    visible = (positions[None, None, :] <= positions[None, :, None]) & (
        seg[:, None, :] == seg[:, :, None]
    )
    visible = visible[:, None]
    row_positions = jnp.broadcast_to(
        positions.reshape(C, 1, rows), (C, micros, rows)
    ).reshape(-1)
    cos_table, sin_table = rotary_tables(row_positions)

    def to_packs(array):
        array = array.reshape(C, micros, rows, heads, HEAD).transpose(1, 3, 0, 2, 4)
        return array.reshape(micros, heads, pack_len, HEAD)

    def from_packs(array):
        array = array.reshape(micros, heads, C, rows, HEAD).transpose(2, 0, 3, 1, 4)
        return array.reshape(total_rows, local_qk)

    def turn(array, sin_signed):
        return rotate(array.reshape(total_rows, heads, HEAD), cos_table, sin_signed)

    def batched(spec, left, right):
        return jnp.einsum(spec, left, right, preferred_element_type=wide)

    all_weights = [layer_weights(layer) for layer in range(layers)]

    kept_layers = []
    own_values = tokens_rows.astype(wide)
    for layer in range(layers):
        qkv, out, up, down, gains, shifts, b_qkv, b_up, b_rest = all_weights[layer]
        unit, _ = normalise(values_all)
        h1 = (unit * gains[0] + shifts[0]).astype(low)
        h2 = (unit * gains[1] + shifts[1]).astype(low)
        mixed = matmul(h1, qkv) + b_qkv
        query = to_packs(turn(mixed[:, :local_qk], sin_table).astype(low))
        key = to_packs(turn(mixed[:, local_qk : 2 * local_qk], sin_table).astype(low))
        value = to_packs(mixed[:, 2 * local_qk :].astype(low))
        scores = batched("mhqd,mhkd->mhqk", query, key) * score_scale
        scores = jnp.where(visible, scores, masked_score)
        peak = jnp.max(scores, axis=-1, keepdims=True)
        exps = jnp.exp(scores - peak)
        soft = exps / jnp.sum(exps, axis=-1, keepdims=True)
        soft_low = soft.astype(low)
        attended = from_packs(batched("mhqk,mhkd->mhqd", soft_low, value).astype(low))
        upward = matmul(h2, up) + b_up
        active = jax.nn.gelu(upward, approximate=False).astype(low)
        change = sum_rows(matmul(attended, out) + matmul(active, down)) + b_rest
        kept_layers.append(
            (values_all, own_values, h1, h2, query, key, value, soft, attended, upward, active)
        )
        own_values = own_values + change
        if layer + 1 < layers:
            values_all = gather_rows(own_values)
    block_out = own_values.astype(low).reshape(micros, 1, rows, width)

    own_grad = cot_rows.astype(wide)
    cot_low = cot_all
    mine = (jnp.arange(C) == place).astype(wide)
    pieces = [None] * layers
    for layer in reversed(range(layers)):
        qkv, out, up, down, gains, shifts, b_qkv, b_up, b_rest = all_weights[layer]
        values, own_in, h1, h2, query, key, value, soft, attended, upward, active = kept_layers[
            layer
        ]
        d_down = matmul_tn(active, cot_low)
        d_out = matmul_tn(attended, cot_low)
        db_rest = jnp.sum(own_grad.astype(low).astype(wide), axis=0)
        d_active = matmul_nt(cot_low, down)
        _, gelu_pull = jax.vjp(lambda u: jax.nn.gelu(u, approximate=False), upward)
        d_upward = gelu_pull(d_active)[0].astype(low)
        d_up = matmul_tn(h2, d_upward)
        db_up = jnp.sum(d_upward.astype(wide), axis=0)
        d_h2 = matmul_nt(d_upward, up)
        d_att = to_packs(matmul_nt(cot_low, out).astype(low))
        d_soft = batched("mhqd,mhkd->mhqk", d_att, value)
        d_value = batched("mhqk,mhqd->mhkd", soft.astype(low), d_att)
        inner = jnp.sum(soft * d_soft, axis=-1, keepdims=True)
        d_scores = (soft * (d_soft - inner)).astype(low)
        d_query = batched("mhqk,mhkd->mhqd", d_scores, key) * score_scale
        d_key = batched("mhqk,mhqd->mhkd", d_scores, query) * score_scale
        d_mixed = jnp.concatenate(
            [
                turn(from_packs(d_query), -sin_table).reshape(total_rows, local_qk),
                turn(from_packs(d_key), -sin_table).reshape(total_rows, local_qk),
                from_packs(d_value),
            ],
            axis=1,
        ).astype(low)
        d_qkv = matmul_tn(h1, d_mixed)
        db_qkv = jnp.sum(d_mixed.astype(wide), axis=0)
        d_h1 = matmul_nt(d_mixed, qkv)
        unit, _ = normalise(values)
        dg = jnp.stack([jnp.sum(d_h1 * unit, axis=0), jnp.sum(d_h2 * unit, axis=0)])
        ds = jnp.stack([jnp.sum(d_h1, axis=0), jnp.sum(d_h2, axis=0)])
        flow = sum_rows(d_h1 * gains[0] + d_h2 * gains[1])
        unit_own, inverse = normalise(own_in)
        flow = flow - jnp.mean(flow, axis=-1, keepdims=True) - unit_own * jnp.mean(
            flow * unit_own, axis=-1, keepdims=True
        )
        own_grad = own_grad + inverse * flow
        if layer > 0:
            cot_low = gather_rows(own_grad.astype(low))

        db_qkv = (db_qkv.reshape(3, 1, local_qk) * mine[None, :, None]).reshape(-1)
        db_up = (db_up.reshape(F, 1, hidden) * mine[None, :, None]).reshape(-1)
        db = jnp.concatenate([db_qkv, db_rest, db_rest, db_up]).reshape(F * C, own_bias)
        dg = dg.reshape(2, F * C, depth).transpose(1, 0, 2).reshape(F * C, 2 * depth)
        ds = ds.reshape(2, F * C, depth).transpose(1, 0, 2).reshape(F * C, 2 * depth)
        small = jnp.concatenate(
            [db, dg, ds, jnp.zeros((F * C, small_pad - own_small), wide)], axis=1
        )
        payload = jnp.concatenate(
            slabs(d_qkv.reshape(F, C * depth, 3 * local_qk).astype(low))
            + slabs(d_up.reshape(F, C * depth, local_ff).astype(low))
            + slabs(d_down.reshape(F, hidden, width).astype(low))
            + slabs(d_out.reshape(F, out_rows, width).astype(low))
            + [small.astype(low).reshape(F, -1, LANES)],
            axis=1,
        )
        parts = lax.all_to_all(payload, "fsdp", 0, 0, tiled=False)
        pieces[layer] = jnp.sum(parts.astype(wide), axis=0)
    grad_tokens = own_grad.reshape(micros, 1, rows, width)

    merged = jnp.stack(pieces)
    n_cols = column_slabs * C * depth
    n_down = width // LANES * hidden
    n_out = width // LANES * out_rows
    cols = merged[:, :n_cols].reshape(layers, column_slabs, C, depth, LANES)
    cols = cols.transpose(2, 0, 1, 3, 4).reshape(C, layers, -1, LANES)
    small = merged[:, n_cols + n_down + n_out :].reshape(layers, C, -1, LANES).transpose(1, 0, 2, 3)
    home = lax.all_to_all(jnp.concatenate([cols, small], axis=2), "ctx", 0, 0, tiled=False)
    down_sum = merged[:, n_cols : n_cols + n_down].reshape(layers, -1, hidden, LANES)
    grad_down = down_sum.transpose(0, 2, 1, 3).reshape(layers, hidden, width)
    out_sum = merged[:, n_cols + n_down : n_cols + n_down + n_out]
    out_sum = out_sum.reshape(layers, -1, out_rows, LANES).transpose(0, 2, 1, 3)
    grad_out = lax.ppermute(out_sum.reshape(layers, out_rows, width), ("fsdp", "ctx"), back)

    n_own = column_slabs * depth
    columns = home[:, :, :n_own].reshape(C, layers, column_slabs, depth, LANES)
    grad_qkv = columns[:, :, :3].transpose(1, 3, 2, 0, 4).reshape(layers, depth, 3 * width)
    grad_up = columns[:, :, 3:].transpose(0, 1, 3, 2, 4).reshape(C, layers, depth, F, hidden)
    grad_up = grad_up.transpose(1, 2, 3, 0, 4).reshape(layers, depth, F * C * hidden)
    small = jnp.sum(home[:, :, n_own:], axis=0).reshape(layers, small_pad)
    grad_bias = small[:, :own_bias]
    grad_gain = small[:, own_bias : own_bias + 2 * depth].reshape(layers, 2, depth)
    grad_shift = small[:, own_bias + 2 * depth : own_small].reshape(layers, 2, depth)
    return (
        block_out,
        grad_tokens,
        grad_qkv,
        grad_out,
        grad_up,
        grad_down,
        grad_gain,
        grad_shift,
        grad_bias,
    )


def solution(mesh):
    weight = P(None, ("fsdp", "ctx"), None)
    rows = P(None, "fsdp", "ctx", None)
    feature = P(None, None, ("fsdp", "ctx"))
    flat = P(None, ("fsdp", "ctx"))
    return jax.shard_map(
        body,
        mesh=mesh,
        in_specs=(
            rows,
            rows,
            P(None, "fsdp", None),
            weight,
            weight,
            weight,
            weight,
            feature,
            feature,
            flat,
        ),
        out_specs=(rows, rows, weight, weight, weight, weight, feature, feature, flat),
        check_vma=False,
    )
```

time: 2180 us -> 486 us (0.22); the launches traced: 2150 us -> 480 us
  waiting for transfers between devices: 1510 us -> 137 us
  blocking collectives: 370 us -> 8.45 us
  local copies, waits for them, and re-layouts: 93 us -> 156 us
  matrix products: 108 us -> 50.1 us
  starting transfers between devices: 1.71 us -> 51.8 us
    reduce_scatter x16 -> x0, waiting for transfers between devices: 1090 us -> none  [the longest x2 277 us: body(): lax.psum_scatter(layer_sums[2], ('fsdp', 'ctx'), scatter_dimension=0, til...]
    unnamed x30 -> x3, waiting for transfers between devices: 416 us -> 0.05 us
    all_gather x14 -> x1, blocking collectives: 278 us -> 8.45 us  [gather_rows(): return lax.all_gather(own, 'ctx', axis=0).reshape(total_rows, width)]
    unnamed x2 -> x0, blocking collectives: 92.7 us -> none
    all_to_all x0 -> x9, waiting for transfers between devices: none -> 70 us  [the longest x2 61.1 us: body(): parts = lax.all_to_all(payload, 'fsdp', 0, 0, tiled=False)]
    all_gather x6 -> x3, waiting for transfers between devices: 0.09 us -> 59.4 us  [the longest x1 56 us: layer_weights(): gathered = lax.all_gather(payload, 'fsdp', axis=0)]
    all_to_all x0 -> x9, starting transfers between devices: none -> 44.2 us  [the longest x4 20 us: sum_rows(): parts = lax.all_to_all(parts, 'ctx', 0, 0, tiled=False)]
    dot_general x40 -> x18, matrix products: 49.6 us -> 25.1 us  [the longest x10 13.6 us: batched(): return jnp.einsum(spec, left, right, preferred_element_type=wide)]
  transfers between devices with their start and end apart: 26 -> 14, of which waited for: 17 -> 8; matrix products, arithmetic and copies ran while one was open for 11% -> 28% of each run, Pallas kernels for 0% -> 0%
where the time goes in v1:
time: 486 us; the launch traced here: 480 us
  local copies, waits for them, and re-layouts  156 us (32%)
  waiting for transfers between devices  137 us (28%)
  other arithmetic  60.6 us (12%)
  starting transfers between devices  51.8 us (11%)
  matrix products  50.1 us (10%)
  between operations  16.5 us (3%)
  blocking collectives  8.45 us (2%)
    all_to_all x2, waiting for transfers between devices, body(): parts = lax.all_to_all(payload, 'fsdp', 0, 0, tiled=False)  61.1 us
    all_gather x1, waiting for transfers between devices, layer_weights(): gathered = lax.all_gather(payload, 'fsdp', axis=0)  56 us
    unnamed x376, local copies, waits for them, and re-layouts  32.4 us
    all_to_all x4, starting transfers between devices, sum_rows(): parts = lax.all_to_all(parts, 'ctx', 0, 0, tiled=False)  20 us
    another operation x8, local copies, waits for them, and re-layouts, body(): active = jax.nn.gelu(upward, approximate=False).astype(low)  15.1 us
    dot_general x10, matrix products, batched(): return jnp.einsum(spec, left, right, preferred_element_type=wide)  13.6 us
    dot_general x8, matrix products, matmul_nt(): lax.dot_general(left, right, (((1,), (1,)), ((), ())), preferred_element_...  13.5 us
    dot_general x8, matrix products, matmul(): return jnp.dot(left, right, preferred_element_type=wide)  11.5 us
  transfers between devices with their start and end apart: 14, of which 8 were waited for; matrix products, arithmetic and copies ran while one was open for 28% of the time, Pallas kernels for 0%

profile of v1, /device:TPU:6, one launch (start us, length us, event | category | flops | bytes accessed | tf_op | source)
XLA Modules:
  0.0 479.6 jit_solution(16608425376300192388)
XLA Ops:
  7.2 5.4 %collective-permute-start = (bf16[2,16,512]{2,1,0:T(8,128)(2,1)}, bf16[2,16,512]{2,1,0:T(8,128)(2,1)S(1)}, u32[]{:S(2)}, u32[]{:S(2)}) collective-permute-start(bf16[2,16,512]{2,1,0:T(8,128)(2,1)} %param.14), channel_id=1, source_target_pairs={{0,0},{1,4},{2,8},{3,12},{4,16},{5,20},{6,24},{7,28},{8,1},{9,5},{... | collective-permute-start | bytes 98312 | tf_op jit(solution)/shard_map/ppermute | solution.py:98
  18.3 3.4 all-to-all-start
  22.6 3.1 all-to-all-done
  29.3 4.9 %all-to-all-start.1 = ((bf16[8,776,128]{2,1,0:T(8,128)(2,1)}), bf16[8,776,128]{2,1,0:T(8,128)(2,1)S(1)}, u32[]{:S(2)}, u32[]{:S(2)}) async-start(bf16[8,776,128]{2,1,0:T(8,128)(2,1)} %broadcast_in_dim.25), calls=%async_computation.1 | async-start | bytes 3178496 | tf_op jit(solution)/shard_map/all_to_all | solution.py:118
  43.5 56.0 %all-gather.10.cloned.1.call-done = bf16[6208,128]{1,0:T(8,128)(2,1)} async-done(((bf16[776,128]{1,0:T(8,128)(2,1)}), bf16[6208,128]{1,0:T(8,128)(2,1)}) %all-gather.10.cloned.1.call-update) | async-done | bytes 1589264 | tf_op jit(solution)/shard_map/all_gather | solution.py:122
  141.4 3.2 fusion.36
  146.3 2.3 fusion.8
  148.6 4.7 all-to-all-start.2
  153.4 3.4 broadcast_subtract_fusion
  160.9 2.0 copy.794
  162.9 2.1 copy.795
  169.3 2.0 copy.804
  173.2 2.6 copy.805
  176.5 1.9 fusion.130
  182.0 2.1 all-gather.6.cloned.1.call-done
  193.1 2.2 fusion.142
  195.2 2.9 convolution_convert_fusion.12
  198.1 2.5 convolution_convert_fusion.6
  212.5 3.4 fusion.37
  215.9 2.6 copy.814
  218.5 2.2 abs_compare_fusion
  220.7 3.3 broadcast_subtract_fusion.1
  223.9 2.1 copy.811
  226.0 2.1 copy.812
  229.9 1.9 copy.776
  235.4 1.9 copy.762
  247.1 2.2 fusion.88
  259.0 2.1 multiply_reduce_fusion.1
  265.3 6.0 %all-to-all-start.4 = ((bf16[4,128,512]{2,1,0:T(8,128)(2,1)}), bf16[4,128,512]{2,1,0:T(8,128)(2,1)}, u32[]{:S(2)}, u32[]{:S(2)}) async-start(bf16[4,128,512]{2,1,0:T(8,128)(2,1)} %bitcast.501), calls=%async_computation.4 | async-start | bytes 1048576 | tf_op jit(solution)/shard_map/all_to_all | solution.py:158
  280.5 2.0 copy.821
  282.5 2.5 copy.819
  286.4 2.6 copy.822
  290.8 2.8 fusion.9
  293.6 4.3 all-to-all-start.3
  300.3 8.4 %all_gather.25 = bf16[4,128,512]{2,1,0:T(8,128)(2,1)S(1)} all-gather(bf16[1,128,512]{2,1,0:T(8,128)(2,1)S(1)} %fusion.57), channel_id=1, replica_groups=mesh['fsdp'=8,'ctx'=4] {'ctx'}, dimensions={0}, use_global_device_ids=true | all-gather | bytes 655360 | tf_op jit(solution)/shard_map/all_gather | solution.py:162
  308.7 3.6 convert_reduce_fusion.7
  314.0 2.5 convolution_convert_fusion.10
  336.8 3.0 multiply_reduce_fusion.3
  351.9 5.1 %all-to-all-start.5 = ((bf16[4,128,512]{2,1,0:T(8,128)(2,1)}), bf16[4,128,512]{2,1,0:T(8,128)(2,1)S(1)}, u32[]{:S(2)}, u32[]{:S(2)}) async-start(bf16[4,128,512]{2,1,0:T(8,128)(2,1)} %bitcast.105), calls=%async_computation.5 | async-start | bytes 1048576 | tf_op jit(solution)/shard_map/all_to_all | solution.py:158
  358.4 5.8 %all-to-all-done.5 = bf16[4,128,512]{2,1,0:T(8,128)(2,1)S(1)} async-done(((bf16[4,128,512]{2,1,0:T(8,128)(2,1)}), bf16[4,128,512]{2,1,0:T(8,128)(2,1)S(1)}, u32[]{:S(2)}, u32[]{:S(2)}) %all-to-all-start.5) | async-done | bytes 524320 | tf_op jit(solution)/shard_map/all_to_all | solution.py:158
  365.1 6.3 %all-to-all-start.6 = ((bf16[8,776,128]{2,1,0:T(8,128)(2,1)}), bf16[8,776,128]{2,1,0:T(8,128)(2,1)}, u32[]{:S(2)}, u32[]{:S(2)}) async-start(bf16[8,776,128]{2,1,0:T(8,128)(2,1)} %constant_dynamic-update-slice_fusion.18), calls=%async_computation.6 | async-start | bytes 3178496 | tf_op jit(solution)/shard_map/all_to_all | solution.py:284
  371.4 2.2 fusion.12
  380.1 28.1 %all-to-all-done.6 = bf16[8,776,128]{2,1,0:T(8,128)(2,1)} async-done(((bf16[8,776,128]{2,1,0:T(8,128)(2,1)}), bf16[8,776,128]{2,1,0:T(8,128)(2,1)}, u32[]{:S(2)}, u32[]{:S(2)}) %all-to-all-start.6) | async-done | bytes 1589280 | tf_op jit(solution)/shard_map/all_to_all | solution.py:284
  408.2 4.8 all-to-all-start.7
  416.4 33.0 %all-to-all-done.7 = bf16[8,776,128]{2,1,0:T(8,128)(2,1)} async-done(((bf16[8,776,128]{2,1,0:T(8,128)(2,1)}), bf16[8,776,128]{2,1,0:T(8,128)(2,1)}, u32[]{:S(2)}, u32[]{:S(2)}) %all-to-all-start.7) | async-done | bytes 1589280 | tf_op jit(solution)/shard_map/all_to_all | solution.py:284
  452.4 4.8 %all-to-all-start.8 = ((f32[4,2,114,128]{3,1,2,0:T(2,128)}), f32[4,2,114,128]{3,1,2,0:T(2,128)S(1)}, u32[]{:S(2)}, u32[]{:S(2)}) async-start(f32[4,2,114,128]{3,1,2,0:T(2,128)} %copy.830), calls=%async_computation.8 | async-start | bytes 933888 | tf_op jit(solution)/shard_map/all_to_all | solution.py:295
  458.2 1.9 collective-permute-start.1
  460.9 7.1 %collective-permute-done.1 = f32[2,16,512]{2,1,0:T(8,128)S(1)} collective-permute-done((f32[2,16,512]{2,1,0:T(8,128)S(1)}, f32[2,16,512]{2,1,0:T(8,128)S(1)}, u32[]{:S(2)}, u32[]{:S(2)}) %collective-permute-start.1) | collective-permute-done | bytes 65568 | tf_op jit(solution)/shard_map/ppermute | solution.py:300
  (715 shorter events, 195.9 us)
Async XLA Ops:
  7.2 15.4 %collective-permute-start = (bf16[2,16,512]{2,1,0:T(8,128)(2,1)}, bf16[2,16,512]{2,1,0:T(8,128)(2,1)S(1)}, u32[]{:S(2)}, u32[]{:S(2)}) collective-permute-start(bf16[2,16,512]{2,1,0:T(8,128)(2,1)} %param.14), channel_id=1, source_target_pairs={{0,0},{1,4},{2,8},{3,12},{4,16},{5,20},{6,24},{7,28},{8,1},{9,5},{... | collective-permute-start | bytes 98312 | tf_op jit(solution)/shard_map/ppermute | solution.py:98
  15.8 5.9 %copy-start.5 = (bf16[2,1,64,512]{3,2,1,0:T(8,128)(2,1)S(1)}, bf16[2,1,64,512]{3,2,1,0:T(8,128)(2,1)}, u32[]{:S(2)}) copy-start(bf16[2,1,64,512]{3,2,1,0:T(8,128)(2,1)} %param.10) | copy-start | bytes 393220
  15.8 5.9 %copy-start.31 = (bf16[2,1,64,512]{3,2,1,0:T(8,128)(2,1)S(1)}, bf16[2,1,64,512]{3,2,1,0:T(8,128)(2,1)}, u32[]{:S(2)}) copy-start(bf16[2,1,64,512]{3,2,1,0:T(8,128)(2,1)} %param.11) | copy-start | bytes 393220
  18.3 7.4 %all-to-all-start = ((bf16[4,2,114,128]{3,1,2,0:T(2,128)(2,1)}), bf16[4,2,114,128]{3,1,2,0:T(2,128)(2,1)S(1)}, u32[]{:S(2)}, u32[]{:S(2)}) async-start(bf16[4,2,114,128]{3,1,2,0:T(2,128)(2,1)} %copy.727), calls=%async_computation | async-start | bytes 466944 | tf_op jit(solution)/shard_map/all_to_all | solution.py:97
  21.7 17.7 %all-gather.8.cloned.1.call-start = ((), (), s32[]{:S(2)}) async-start(), calls=%async_computation.10 | async-start | bytes 1310720 | tf_op jit(solution)/shard_map/all_gather | solution.py:105
  22.5 76.9 %all-gather.10.cloned.1.call-start = ((), (), s32[]{:S(2)}) async-start(), calls=%async_computation.11 | async-start | bytes 1787904 | tf_op jit(solution)/shard_map/all_gather | solution.py:122
  29.3 81.8 %all-to-all-start.1 = ((bf16[8,776,128]{2,1,0:T(8,128)(2,1)}), bf16[8,776,128]{2,1,0:T(8,128)(2,1)S(1)}, u32[]{:S(2)}, u32[]{:S(2)}) async-start(bf16[8,776,128]{2,1,0:T(8,128)(2,1)} %broadcast_in_dim.25), calls=%async_computation.1 | async-start | bytes 3178496 | tf_op jit(solution)/shard_map/all_to_all | solution.py:118
  36.5 99.1 %copy-start.43 = (f32[512,16]{0,1:T(8,128)}, f32[512,16]{0,1:T(8,128)S(1)}, u32[]{:S(2)}) copy-start(f32[512,16]{0,1:T(8,128)S(1)} %get-tuple-element.122) | copy-start | bytes 98308
  36.5 99.1 %copy-start.79 = (f32[512,16]{0,1:T(8,128)}, f32[512,16]{0,1:T(8,128)S(1)}, u32[]{:S(2)}) copy-start(f32[512,16]{0,1:T(8,128)S(1)} %get-tuple-element.121) | copy-start | bytes 98308
  40.6 84.2 %copy-start.2 = (bf16[4,1,128,512]{3,2,1,0:T(8,128)(2,1)}, bf16[4,1,128,512]{3,2,1,0:T(8,128)(2,1)S(1)}, u32[]{:S(2)}) copy-start(bf16[4,1,128,512]{3,2,1,0:T(8,128)(2,1)S(1)} %slice.829) | copy-start | bytes 1572868
  105.2 5.9 %copy-start.62 = (f32[8,4,144]{2,1,0:T(4,128)}, f32[8,4,144]{2,1,0:T(4,128)S(1)}, u32[]{:S(2)}) copy-start(f32[8,4,144]{2,1,0:T(4,128)S(1)} %copy.755) | copy-start | bytes 55300
  124.0 8.3 %copy-start.27 = (bf16[8,4,64,128]{3,0,2,1:T(8,128)(2,1)S(1)}, bf16[8,4,64,128]{3,0,2,1:T(8,128)(2,1)}, u32[]{:S(2)}) copy-start(bf16[8,4,64,128]{3,0,2,1:T(8,128)(2,1)} %slice.816) | copy-start | bytes 1572868
  148.6 17.8 %all-to-all-start.2 = ((bf16[4,128,512]{2,1,0:T(8,128)(2,1)}), bf16[4,128,512]{2,1,0:T(8,128)(2,1)}, u32[]{:S(2)}, u32[]{:S(2)}) async-start(bf16[4,128,512]{2,1,0:T(8,128)(2,1)} %bitcast.464), calls=%async_computation.2 | async-start | bytes 1048576 | tf_op jit(solution)/shard_map/all_to_all | solution.py:158
  153.2 30.9 %all-gather.6.cloned.1.call-start = ((), (), s32[]{:S(2)}) async-start(), calls=%async_computation.9 | async-start | bytes 1310720 | tf_op jit(solution)/shard_map/all_gather | solution.py:162
  179.8 6.1 %copy-start.137 = (f32[512]{0:T(512)S(1)}, f32[512]{0:T(512)}, u32[]{:S(2)}) copy-start(f32[512]{0:T(512)} %mul.553) | copy-start | bytes 6148
  179.8 6.2 %copy-start.138 = (f32[512]{0:T(512)S(1)}, f32[512]{0:T(512)}, u32[]{:S(2)}) copy-start(f32[512]{0:T(512)} %add.308) | copy-start | bytes 6148
  179.8 6.2 %copy-start.139 = (f32[512]{0:T(512)S(1)}, f32[512]{0:T(512)}, u32[]{:S(2)}) copy-start(f32[512]{0:T(512)} %add.300) | copy-start | bytes 6148
  265.3 28.3 %all-to-all-start.4 = ((bf16[4,128,512]{2,1,0:T(8,128)(2,1)}), bf16[4,128,512]{2,1,0:T(8,128)(2,1)}, u32[]{:S(2)}, u32[]{:S(2)}) async-start(bf16[4,128,512]{2,1,0:T(8,128)(2,1)} %bitcast.501), calls=%async_computation.4 | async-start | bytes 1048576 | tf_op jit(solution)/shard_map/all_to_all | solution.py:158
  271.3 13.7 %copy-start.13 = (f32[512,512]{0,1:T(8,128)S(1)}, f32[512,512]{0,1:T(8,128)}, u32[]{:S(2)}) copy-start(f32[512,512]{0,1:T(8,128)} %get-tuple-element.34) | copy-start | bytes 3145732
  293.6 6.3 %copy-start.121 = (f32[2,64]{1,0:T(2,128)S(1)}, f32[2,64]{1,0:T(2,128)}, u32[]{:S(2)}) copy-start(f32[2,64]{1,0:T(2,128)} %copy-done.120) | copy-start | bytes 1540
  293.6 6.3 %copy-start.127 = (f32[2,64]{1,0:T(2,128)S(1)}, f32[2,64]{1,0:T(2,128)}, u32[]{:S(2)}) copy-start(f32[2,64]{1,0:T(2,128)} %copy-done.126) | copy-start | bytes 1540
  293.6 6.5 %copy-start.18 = (f32[1,128,512]{2,1,0:T(8,128)S(1)}, f32[1,128,512]{2,1,0:T(8,128)}, u32[]{:S(2)}) copy-start(f32[1,128,512]{2,1,0:T(8,128)} %fusion.58) | copy-start | bytes 786436
  293.6 6.5 %copy-start.32 = (bf16[2,1,64,512]{3,2,1,0:T(8,128)(2,1)S(1)}, bf16[2,1,64,512]{3,2,1,0:T(8,128)(2,1)}, u32[]{:S(2)}) copy-start(bf16[2,1,64,512]{3,2,1,0:T(8,128)(2,1)} %param.11) | copy-start | bytes 393220
  293.6 6.5 %copy-start.154 = (f32[128]{0:T(128)S(1)}, f32[128]{0:T(128)}, u32[]{:S(2)}) copy-start(f32[128]{0:T(128)} %div.91) | copy-start | bytes 1540
  293.6 6.5 %copy-start.155 = (f32[128]{0:T(128)S(1)}, f32[128]{0:T(128)}, u32[]{:S(2)}) copy-start(f32[128]{0:T(128)} %rsqrt.50) | copy-start | bytes 1540
  293.6 58.3 %all-to-all-start.3 = ((bf16[4,128,512]{2,1,0:T(8,128)(2,1)}), bf16[4,128,512]{2,1,0:T(8,128)(2,1)}, u32[]{:S(2)}, u32[]{:S(2)}) async-start(bf16[4,128,512]{2,1,0:T(8,128)(2,1)} %bitcast.463), calls=%async_computation.3 | async-start | bytes 1048576 | tf_op jit(solution)/shard_map/all_to_all | solution.py:158
  300.0 27.6 %copy-start.129 = (f32[2,64]{1,0:T(2,128)}, f32[2,64]{1,0:T(2,128)S(1)}, u32[]{:S(2)}) copy-start(f32[2,64]{1,0:T(2,128)S(1)} %broadcast_multiply_fusion.5) | copy-start | bytes 1540
  321.7 5.9 %copy-start.146 = (f32[2,64]{1,0:T(2,128)S(1)}, f32[2,64]{1,0:T(2,128)}, u32[]{:S(2)}) copy-start(f32[2,64]{1,0:T(2,128)} %div.87) | copy-start | bytes 1540
  339.8 7.5 %copy-start.20 = (bf16[8,64,512]{2,1,0:T(8,128)(2,1)S(1)}, bf16[8,64,512]{2,1,0:T(8,128)(2,1)}, u32[]{:S(2)}) copy-start(bf16[8,64,512]{2,1,0:T(8,128)(2,1)} %convolution_convert_fusion.2) | copy-start | bytes 1572868
  341.5 8.6 %copy-start.60 = (bf16[8,16,512]{2,1,0:T(8,128)(2,1)S(1)}, bf16[8,16,512]{2,1,0:T(8,128)(2,1)}, u32[]{:S(2)}) copy-start(bf16[8,16,512]{2,1,0:T(8,128)(2,1)} %convolution_convert_fusion.9) | copy-start | bytes 393220
  345.2 11.8 %copy-start.118 = (bf16[32,32]{1,0:T(8,128)(2,1)S(1)}, bf16[32,32]{1,0:T(8,128)(2,1)}, u32[]{:S(2)}) copy-start(bf16[32,32]{1,0:T(8,128)(2,1)} %copy.826) | copy-start | bytes 6148
  345.2 11.8 %copy-start.119 = (bf16[32,32]{1,0:T(8,128)(2,1)S(1)}, bf16[32,32]{1,0:T(8,128)(2,1)}, u32[]{:S(2)}) copy-start(bf16[32,32]{1,0:T(8,128)(2,1)} %copy.827) | copy-start | bytes 6148
  345.2 11.8 %copy-start.153 = (bf16[256]{0:T(256)(128)(2,1)S(1)}, bf16[256]{0:T(256)(128)(2,1)}, u32[]{:S(2)}) copy-start(bf16[256]{0:T(256)(128)(2,1)} %pad.24.clone) | copy-start | bytes 1540
  351.9 12.3 %all-to-all-start.5 = ((bf16[4,128,512]{2,1,0:T(8,128)(2,1)}), bf16[4,128,512]{2,1,0:T(8,128)(2,1)S(1)}, u32[]{:S(2)}, u32[]{:S(2)}) async-start(bf16[4,128,512]{2,1,0:T(8,128)(2,1)} %bitcast.105), calls=%async_computation.5 | async-start | bytes 1048576 | tf_op jit(solution)/shard_map/all_to_all | solution.py:158
  358.4 12.9 %copy-start.6 = (f32[512,512]{1,0:T(8,128)S(1)}, f32[512,512]{1,0:T(8,128)}, u32[]{:S(2)}) copy-start(f32[512,512]{1,0:T(8,128)} %copy.819) | copy-start | bytes 3145732
  358.4 13.0 %copy-start.35 = (pred[512,512]{1,0:T(8,128)(4,1)S(1)}, pred[512,512]{1,0:T(8,128)(4,1)}, u32[]{:S(2)}) copy-start(pred[512,512]{1,0:T(8,128)(4,1)} %copy.821) | copy-start | bytes 786436
  365.1 43.2 %all-to-all-start.6 = ((bf16[8,776,128]{2,1,0:T(8,128)(2,1)}), bf16[8,776,128]{2,1,0:T(8,128)(2,1)}, u32[]{:S(2)}, u32[]{:S(2)}) async-start(bf16[8,776,128]{2,1,0:T(8,128)(2,1)} %constant_dynamic-update-slice_fusion.18), calls=%async_computation.6 | async-start | bytes 3178496 | tf_op jit(solution)/shard_map/all_to_all | solution.py:284
  380.1 32.9 %copy-start.63 = (f32[8,4,144]{2,1,0:T(4,128)S(1)}, f32[8,4,144]{2,1,0:T(4,128)}, u32[]{:S(2)}) copy-start(f32[8,4,144]{2,1,0:T(4,128)} %copy-done.62) | copy-start | bytes 55300
  380.1 33.0 %copy-start.145 = (f32[2,64]{1,0:T(2,128)S(1)}, f32[2,64]{1,0:T(2,128)}, u32[]{:S(2)}) copy-start(f32[2,64]{1,0:T(2,128)} %get-tuple-element.95) | copy-start | bytes 1540
  380.1 34.2 %copy-start.29 = (bf16[4,128,512]{2,1,0:T(8,128)(2,1)S(1)}, bf16[4,128,512]{2,1,0:T(8,128)(2,1)}, u32[]{:S(2)}) copy-start(bf16[4,128,512]{2,1,0:T(8,128)(2,1)} %copy-done.28) | copy-start | bytes 1572868
  408.2 41.3 %all-to-all-start.7 = ((bf16[8,776,128]{2,1,0:T(8,128)(2,1)}), bf16[8,776,128]{2,1,0:T(8,128)(2,1)}, u32[]{:S(2)}, u32[]{:S(2)}) async-start(bf16[8,776,128]{2,1,0:T(8,128)(2,1)} %constant_dynamic-update-slice_fusion.23), calls=%async_computation.7 | async-start | bytes 3178496 | tf_op jit(solution)/shard_map/all_to_all | solution.py:284
  451.3 6.0 %copy-start.33 = (bf16[2,1,64,512]{3,2,1,0:T(8,128)(2,1)S(1)}, bf16[2,1,64,512]{3,2,1,0:T(8,128)(2,1)}, u32[]{:S(2)}) copy-start(bf16[2,1,64,512]{3,2,1,0:T(8,128)(2,1)} %param.11) | copy-start | bytes 393220
  451.3 6.0 %copy-start.122 = (f32[2,64]{1,0:T(2,128)S(1)}, f32[2,64]{1,0:T(2,128)}, u32[]{:S(2)}) copy-start(f32[2,64]{1,0:T(2,128)} %copy-done.120) | copy-start | bytes 1540
  451.3 5.9 %copy-start.128 = (f32[2,64]{1,0:T(2,128)S(1)}, f32[2,64]{1,0:T(2,128)}, u32[]{:S(2)}) copy-start(f32[2,64]{1,0:T(2,128)} %copy-done.126) | copy-start | bytes 1540
  451.3 5.9 %copy-start.130 = (f32[2,64]{1,0:T(2,128)S(1)}, f32[2,64]{1,0:T(2,128)}, u32[]{:S(2)}) copy-start(f32[2,64]{1,0:T(2,128)} %copy-done.129) | copy-start | bytes 1540
  451.3 5.9 %copy-start.147 = (f32[2,64]{1,0:T(2,128)S(1)}, f32[2,64]{1,0:T(2,128)}, u32[]{:S(2)}) copy-start(f32[2,64]{1,0:T(2,128)} %div.87) | copy-start | bytes 1540
  452.4 15.6 %all-to-all-start.8 = ((f32[4,2,114,128]{3,1,2,0:T(2,128)}), f32[4,2,114,128]{3,1,2,0:T(2,128)S(1)}, u32[]{:S(2)}, u32[]{:S(2)}) async-start(f32[4,2,114,128]{3,1,2,0:T(2,128)} %copy.830), calls=%async_computation.8 | async-start | bytes 933888 | tf_op jit(solution)/shard_map/all_to_all | solution.py:295
  458.2 9.8 %collective-permute-start.1 = (f32[2,16,512]{2,1,0:T(8,128)S(1)}, f32[2,16,512]{2,1,0:T(8,128)S(1)}, u32[]{:S(2)}, u32[]{:S(2)}) collective-permute-start(f32[2,16,512]{2,1,0:T(8,128)S(1)} %bitcast.582), channel_id=1, source_target_pairs={{0,0},{4,1},{8,2},{12,3},{16,4},{20,5},{24,6},{28,7},{1,8},{5,9},{... | collective-permute-start | bytes 196616 | tf_op jit(solution)/shard_map/ppermute | solution.py:300
  (126 other events, 340.2 us)
Sparse Core Ops, SparseCore 0:
  24.6 14.7 all-gather.7
  42.2 57.2 all-gather.9
  168.5 15.5 all-gather.5

commit v2 on v1

v2 whole, which is shorter than its diff:
```python
import functools

import jax
import jax.numpy as jnp
from jax import lax
from jax.experimental import pallas as pl
from jax.experimental.pallas import tpu as pltpu
from jax.sharding import PartitionSpec as P

HEAD = 64
LANES = 128

masked_score = -1e30
norm_eps = 1e-05
low = jnp.bfloat16
wide = jnp.float32


def matmul(left, right):
    return jnp.dot(left, right, preferred_element_type=wide)


def matmul_tn(left, right):
    return lax.dot_general(left, right, (((0,), (0,)), ((), ())), preferred_element_type=wide)


def matmul_nt(left, right):
    return lax.dot_general(left, right, (((1,), (1,)), ((), ())), preferred_element_type=wide)


def normalise(values):
    centred = values - jnp.mean(values, axis=-1, keepdims=True)
    inverse = lax.rsqrt(jnp.mean(centred * centred, axis=-1, keepdims=True) + norm_eps)
    return centred * inverse, inverse


def rotary_tables(positions, columns):
    lane = jnp.arange(columns, dtype=jnp.int32) % HEAD
    frequency = 10000.0 ** (-(lane % 8).astype(wide) / 8.0)
    angles = positions.astype(wide)[:, None] * frequency[None, :]
    cos, sin = jnp.cos(angles), jnp.sin(angles)
    return jnp.stack(
        [
            jnp.where(lane < 16, cos, 1.0),
            jnp.where((lane >= 8) & (lane < 16), sin, 0.0),
            jnp.where(lane < 8, -sin, 0.0),
        ]
    )


def turned(array, own, before, after):
    return (
        array * own
        + pltpu.roll(array, 8, 1) * before
        + pltpu.roll(array, array.shape[1] - 8, 1) * after
    )


def pack_rows(array, micro, micros, places):
    rows = array.shape[0] // (micros * places)
    starts = [(place * micros + micro) * rows for place in range(places)]
    return jnp.concatenate([array[start : start + rows] for start in starts], axis=0)


def put_rows(ref, columns, array, micro, micros, places):
    rows = array.shape[0] // places
    for place in range(places):
        start = (place * micros + micro) * rows
        ref[start : start + rows, columns] = array[place * rows : (place + 1) * rows]


def phi_of(upward):
    return 0.5 * (1.0 + lax.erf(upward * (0.5**0.5)))


def forward_kernel(
    micros,
    places,
    x_ref,
    qkv_ref,
    out_ref,
    up_ref,
    down_ref,
    gain_ref,
    shift_ref,
    b_qkv_ref,
    b_up_ref,
    table_ref,
    visible_ref,
    change_ref,
    h1_ref,
    h2_ref,
    mixed_ref,
    soft_ref,
    att_ref,
    upward_ref,
    active_ref,
):
    local = out_ref.shape[0]
    heads = local // HEAD
    unit, _ = normalise(x_ref[...])
    h1_ref[...] = (unit * gain_ref[0:1] + shift_ref[0:1]).astype(low)
    h2_ref[...] = (unit * gain_ref[1:2] + shift_ref[1:2]).astype(low)
    mixed = matmul(h1_ref[...], qkv_ref[...]) + b_qkv_ref[...]
    tables = [table_ref[i] for i in range(3)]
    mixed_ref[:, :local] = turned(mixed[:, :local], *tables).astype(low)
    mixed_ref[:, local : 2 * local] = turned(mixed[:, local : 2 * local], *tables).astype(low)
    mixed_ref[:, 2 * local :] = mixed[:, 2 * local :].astype(low)
    lane = lax.broadcasted_iota(jnp.int32, (1, local), 1) // HEAD
    for micro in range(micros):
        whole = pack_rows(mixed_ref[...], micro, micros, places)
        query, key, value = (whole[:, i * local : (i + 1) * local] for i in range(3))
        seen = visible_ref[micro] > 0.5
        attended = jnp.zeros((whole.shape[0], local), wide)
        for head in range(heads):
            here = lane == head
            scores = matmul_nt(jnp.where(here, query, jnp.zeros_like(query)), key)
            scores = jnp.where(seen, scores * HEAD**-0.5, masked_score)
            exps = jnp.exp(scores - jnp.max(scores, axis=-1, keepdims=True))
            soft = exps / jnp.sum(exps, axis=-1, keepdims=True)
            soft_ref[micro * heads + head] = soft
            attended = jnp.where(here, matmul(soft.astype(low), value), attended)
        put_rows(att_ref, slice(0, local), attended.astype(low), micro, micros, places)
    upward = matmul(h2_ref[...], up_ref[...]) + b_up_ref[...]
    upward_ref[...] = upward
    active_ref[...] = (upward * phi_of(upward)).astype(low)
    change_ref[...] = (
        matmul(att_ref[...], out_ref[...]) + matmul(active_ref[...], down_ref[...])
    ).astype(low)


def backward_kernel(
    micros,
    places,
    cot_ref,
    x_ref,
    qkv_ref,
    out_ref,
    up_ref,
    down_ref,
    gain_ref,
    table_ref,
    h1_ref,
    h2_ref,
    mixed_ref,
    soft_ref,
    att_ref,
    upward_ref,
    active_ref,
    flow_ref,
    d_qkv_ref,
    d_out_ref,
    d_up_ref,
    d_down_ref,
    db_qkv_ref,
    db_up_ref,
    dg_ref,
    ds_ref,
    d_turned,
    d_mixed,
):
    local = out_ref.shape[0]
    heads = local // HEAD
    cot = cot_ref[...]
    d_att = matmul_nt(cot, out_ref[...]).astype(low)
    lane = lax.broadcasted_iota(jnp.int32, (1, local), 1) // HEAD
    for micro in range(micros):
        whole = pack_rows(mixed_ref[...], micro, micros, places)
        query, key, value = (whole[:, i * local : (i + 1) * local] for i in range(3))
        d_own = pack_rows(d_att, micro, micros, places)
        d_query = jnp.zeros(query.shape, wide)
        d_key, d_value = d_query, d_query
        for head in range(heads):
            here = lane == head
            soft = soft_ref[micro * heads + head]
            d_soft = matmul_nt(jnp.where(here, d_own, jnp.zeros_like(d_own)), value)
            d_value = jnp.where(here, matmul_tn(soft.astype(low), d_own), d_value)
            inner = jnp.sum(soft * d_soft, axis=-1, keepdims=True)
            d_scores = (soft * (d_soft - inner)).astype(low)
            d_query = jnp.where(here, matmul(d_scores, key), d_query)
            d_key = jnp.where(here, matmul_tn(d_scores, query), d_key)
        scale = HEAD**-0.5
        put_rows(d_turned, slice(0, local), d_query * scale, micro, micros, places)
        put_rows(d_turned, slice(local, 2 * local), d_key * scale, micro, micros, places)
        put_rows(d_turned, slice(2 * local, 3 * local), d_value, micro, micros, places)
    tables = (table_ref[0], -table_ref[1], -table_ref[2])
    d_mixed[:, :local] = turned(d_turned[:, :local], *tables).astype(low)
    d_mixed[:, local : 2 * local] = turned(d_turned[:, local : 2 * local], *tables).astype(low)
    d_mixed[:, 2 * local :] = d_turned[:, 2 * local :].astype(low)
    d_qkv_ref[...] = matmul_tn(h1_ref[...], d_mixed[...]).astype(low)
    db_qkv_ref[...] = jnp.sum(d_mixed[...].astype(wide), axis=0, keepdims=True)
    d_down_ref[...] = matmul_tn(active_ref[...], cot).astype(low)
    d_out_ref[...] = matmul_tn(att_ref[...], cot).astype(low)
    upward = upward_ref[...]
    slope = phi_of(upward) + upward * (jnp.exp(-0.5 * upward * upward) * 0.3989422804014327)
    d_upward = (matmul_nt(cot, down_ref[...]) * slope).astype(low)
    d_up_ref[...] = matmul_tn(h2_ref[...], d_upward).astype(low)
    db_up_ref[...] = jnp.sum(d_upward.astype(wide), axis=0, keepdims=True)
    unit, _ = normalise(x_ref[...])
    d_h1 = matmul_nt(d_mixed[...], qkv_ref[...])
    dg_ref[0:1] = jnp.sum(d_h1 * unit, axis=0, keepdims=True)
    ds_ref[0:1] = jnp.sum(d_h1, axis=0, keepdims=True)
    d_h2 = matmul_nt(d_upward, up_ref[...])
    dg_ref[1:2] = jnp.sum(d_h2 * unit, axis=0, keepdims=True)
    ds_ref[1:2] = jnp.sum(d_h2, axis=0, keepdims=True)
    flow_ref[...] = (d_h1 * gain_ref[0:1] + d_h2 * gain_ref[1:2]).astype(low)


def assemble_kernel(places, gathered_ref, qkv_ref, out_ref, up_ref, down_ref):
    shards = gathered_ref.shape[0]
    depth = qkv_ref.shape[0] // (shards * places)
    hidden, out_rows = down_ref.shape[0] // shards, out_ref.shape[0] // shards
    for shard in range(shards):
        start = 0
        for place in range(places):
            first = (shard * places + place) * depth
            for target in (qkv_ref, up_ref):
                for left in range(0, target.shape[1], LANES):
                    target[first : first + depth, left : left + LANES] = gathered_ref[
                        shard, start : start + depth
                    ]
                    start += depth
        for target, size in ((down_ref, hidden), (out_ref, out_rows)):
            for left in range(0, target.shape[1], LANES):
                target[shard * size : (shard + 1) * size, left : left + LANES] = gathered_ref[
                    shard, start : start + size
                ]
                start += size


def pack_kernel(qkv_ref, up_ref, down_ref, out_ref, small_ref, payload_ref):
    shards = payload_ref.shape[0]
    for shard in range(shards):
        start = 0
        for source in (qkv_ref, up_ref, down_ref, out_ref):
            size = source.shape[0] // shards
            for left in range(0, source.shape[1], LANES):
                payload_ref[shard, start : start + size] = source[
                    shard * size : (shard + 1) * size, left : left + LANES
                ]
                start += size
        payload_ref[shard, start : start + small_ref.shape[1]] = small_ref[shard]


def call(kernel, outs, scratch, *args):
    return pl.pallas_call(
        kernel,
        out_shape=[jax.ShapeDtypeStruct(shape, kind) for shape, kind in outs],
        in_specs=[pl.BlockSpec(memory_space=pltpu.VMEM)] * len(args),
        out_specs=[pl.BlockSpec(memory_space=pltpu.VMEM)] * len(outs),
        scratch_shapes=[pltpu.VMEM(shape, kind) for shape, kind in scratch],
        compiler_params=pltpu.CompilerParams(vmem_limit_bytes=40 * 1024 * 1024),
        cost_estimate=pl.CostEstimate(
            flops=3_000_000_000, bytes_accessed=10_000_000, transcendentals=1_000_000
        ),
    )(*args)


def segments_of(lengths, positions):
    endings = jnp.cumsum(lengths, axis=-1)
    return jnp.sum((endings[:, None, :] <= positions[None, :, None]).astype(jnp.int32), axis=-1)


def slabs(array):
    pieces = array.shape[-1] // LANES
    return [array[..., LANES * i : LANES * (i + 1)] for i in range(pieces)]


def body(
    tokens, cotangent, doc_lengths, w_qkv, w_out, w_up, w_down, norm_gain, norm_bias, proj_bias
):
    micros, _, rows, width = tokens.shape
    layers = w_qkv.shape[0]
    C = lax.axis_size("ctx")
    F = lax.axis_size("fsdp")
    place = lax.axis_index("ctx")
    hidden = w_down.shape[1]
    depth = w_qkv.shape[1]
    local_qk = width // C
    heads = local_qk // HEAD
    local_ff = F * hidden
    pack_len = rows * C
    total_rows = C * micros * rows
    score_scale = HEAD ** (-0.5)
    own_bias = proj_bias.shape[1]
    own_small = own_bias + 4 * depth
    small_pad = -(-own_small // LANES) * LANES
    out_rows = local_qk // F

    forth = [(b, (b % F) * C + b // F) for b in range(F * C)]
    back = [(there, here) for here, there in forth]

    small_own = jnp.concatenate(
        [proj_bias, norm_gain.reshape(layers, -1), norm_bias.reshape(layers, -1)], axis=1
    )
    small_own = jnp.pad(small_own, ((0, 0), (0, small_pad - own_small)))
    qkv_cols = w_qkv.reshape(layers, depth, 3, C, local_qk).transpose(3, 0, 2, 1, 4)
    up_cols = w_up.reshape(layers, depth, F, C, hidden).transpose(3, 0, 1, 2, 4)
    up_cols = up_cols.reshape(C, layers, depth, local_ff // LANES, LANES).transpose(0, 1, 3, 2, 4)
    spread = jnp.concatenate(
        [
            qkv_cols.reshape(C, layers, -1, LANES),
            up_cols.reshape(C, layers, -1, LANES),
            jnp.broadcast_to(
                small_own.reshape(1, layers, -1, LANES), (C, layers, small_pad // LANES, LANES)
            ),
        ],
        axis=2,
    )
    arrived = lax.all_to_all(spread, "ctx", 0, 0, tiled=False)
    w_out_here = lax.ppermute(w_out, ("fsdp", "ctx"), forth)
    aligned = depth % 16 == 0 and hidden % 16 == 0 and out_rows % 16 == 0
    n_qkv = 3 * depth
    n_up = local_ff // LANES * depth
    column_slabs = 3 + local_ff // LANES

    tokens_rows = tokens.reshape(micros * rows, width)
    cot_rows = cotangent.reshape(micros * rows, width)
    values_all = lax.all_gather(tokens_rows, "ctx", axis=0).reshape(total_rows, width)
    values_all = values_all.astype(wide)
    cot_all = lax.all_gather(cot_rows, "ctx", axis=0).reshape(total_rows, width)

    def gather_layer(layer):
        part = arrived[:, layer]
        payload = jnp.concatenate(
            [part[:, : n_qkv + n_up].reshape(-1, LANES)]
            + slabs(w_down[layer])
            + slabs(w_out_here[layer])
            + [part[:, n_qkv + n_up :].reshape(-1, LANES)],
            axis=0,
        )
        size = payload.shape[0]
        if layer == 0:
            return lax.all_to_all(
                jnp.broadcast_to(payload[None], (F, size, LANES)), "fsdp", 0, 0, tiled=False
            )
        return lax.all_gather(payload, "fsdp", axis=0)

    def layer_weights(gathered):
        n_small = C * small_pad // LANES
        n_part = C * (n_qkv + n_up)
        n_down = width // LANES * hidden
        if aligned:
            qkv, out, up, down = call(
                functools.partial(assemble_kernel, C),
                [
                    ((width, 3 * local_qk), low),
                    ((local_qk, width), low),
                    ((width, local_ff), low),
                    ((local_ff, width), low),
                ],
                [],
                gathered,
            )
        else:
            columns = gathered[:, :n_part].reshape(F, C, -1, LANES)
            qkv = columns[:, :, :n_qkv].reshape(F, C, 3, depth, LANES)
            qkv = jnp.concatenate([qkv[:, :, i].reshape(width, LANES) for i in range(3)], axis=1)
            up = columns[:, :, n_qkv:].reshape(F, C, -1, depth, LANES)
            up = [up[:, :, i].reshape(width, LANES) for i in range(local_ff // LANES)]
            up = jnp.concatenate(up, axis=1)
            down = gathered[:, n_part : n_part + n_down].reshape(F, -1, hidden, LANES)
            down = [down[:, i].reshape(local_ff, LANES) for i in range(width // LANES)]
            down = jnp.concatenate(down, axis=1)
            out = gathered[:, n_part + n_down : -n_small].reshape(F, -1, out_rows, LANES)
            out = [out[:, i].reshape(local_qk, LANES) for i in range(width // LANES)]
            out = jnp.concatenate(out, axis=1)
        small = gathered[:, -n_small:].reshape(F, C, small_pad).astype(wide)
        biases = small[:, :, :own_bias].reshape(-1)
        gains = small[:, :, own_bias : own_bias + 2 * depth].reshape(F * C, 2, depth)
        gains = gains.transpose(1, 0, 2).reshape(2, width)
        shifts = small[:, :, own_bias + 2 * depth : own_small].reshape(F * C, 2, depth)
        shifts = shifts.transpose(1, 0, 2).reshape(2, width)
        b_qkv = biases[: 3 * width].reshape(3, C, local_qk)
        b_qkv = lax.dynamic_slice_in_dim(b_qkv, place, 1, 1).reshape(-1)
        b_up = biases[5 * width :].reshape(F, C, hidden)
        b_up = lax.dynamic_slice_in_dim(b_up, place, 1, 1).reshape(-1)
        b_rest = biases[3 * width : 4 * width] + biases[4 * width : 5 * width]
        return (
            qkv,
            out,
            up,
            down,
            gains,
            shifts,
            b_qkv[None],
            b_up[None],
            b_rest,
        )

    def sum_rows(partial):
        parts = partial.reshape(C, micros * rows, width)
        parts = lax.all_to_all(parts, "ctx", 0, 0, tiled=False)
        return jnp.sum(parts.astype(wide), axis=0)

    def gather_rows(own):
        return lax.all_gather(own, "ctx", axis=0).reshape(total_rows, width)

    positions = jnp.arange(pack_len, dtype=jnp.int32)
    seg = segments_of(doc_lengths[:, 0], positions)
    visible = (positions[None, None, :] <= positions[None, :, None]) & (
        seg[:, None, :] == seg[:, :, None]
    )
    visible = visible.astype(wide)
    row_positions = jnp.broadcast_to(positions.reshape(C, 1, rows), (C, micros, rows))
    tables = rotary_tables(row_positions.reshape(-1), local_qk)
    square = (micros * heads, pack_len, pack_len)
    forward_outs = [
        ((total_rows, width), low),
        ((total_rows, width), low),
        ((total_rows, width), low),
        ((total_rows, 3 * local_qk), low),
        (square, wide),
        ((total_rows, local_qk), low),
        ((total_rows, local_ff), wide),
        ((total_rows, local_ff), low),
    ]
    backward_outs = [
        ((total_rows, width), low),
        ((width, 3 * local_qk), low),
        ((local_qk, width), low),
        ((width, local_ff), low),
        ((local_ff, width), low),
        ((1, 3 * local_qk), wide),
        ((1, local_ff), wide),
        ((2, width), wide),
        ((2, width), wide),
    ]
    backward_scratch = [((total_rows, 3 * local_qk), wide), ((total_rows, 3 * local_qk), low)]

    kept_layers = []
    all_weights = []
    gathered = [gather_layer(layer) for layer in range(layers)]
    own_values = tokens_rows.astype(wide)
    for layer in range(layers):
        if layer > 0:
            gathered[layer], values_all = lax.optimization_barrier((gathered[layer], values_all))
        weights = layer_weights(gathered[layer])
        all_weights.append(weights)
        qkv, out, up, down, gains, shifts, b_qkv, b_up, b_rest = weights
        change, *kept = call(
            functools.partial(forward_kernel, micros, C),
            forward_outs,
            [],
            values_all,
            qkv,
            out,
            up,
            down,
            gains,
            shifts,
            b_qkv,
            b_up,
            tables,
            visible,
        )
        kept_layers.append((values_all, own_values, kept))
        change = sum_rows(change) + b_rest
        if layer + 1 < layers:
            change = change.astype(low)
            values_all = values_all + gather_rows(change).astype(wide)
            change = change.astype(wide)
        own_values = own_values + change
    block_out = own_values.astype(low).reshape(micros, 1, rows, width)

    own_grad = cot_rows.astype(wide)
    cot_low = cot_all
    mine = (jnp.arange(C) == place).astype(wide)
    pieces = [None] * layers
    for layer in reversed(range(layers)):
        qkv, out, up, down, gains, shifts, b_qkv, b_up, b_rest = all_weights[layer]
        values, own_in, kept = kept_layers[layer]
        db_rest = jnp.sum(own_grad.astype(low).astype(wide), axis=0)
        flow, d_qkv, d_out, d_up, d_down, db_qkv, db_up, dg, ds = call(
            functools.partial(backward_kernel, micros, C),
            backward_outs,
            backward_scratch,
            cot_low,
            values,
            qkv,
            out,
            up,
            down,
            gains,
            tables,
            *kept,
        )
        flow = sum_rows(flow)
        unit_own, inverse = normalise(own_in)
        flow = flow - jnp.mean(flow, axis=-1, keepdims=True) - unit_own * jnp.mean(
            flow * unit_own, axis=-1, keepdims=True
        )
        own_grad = own_grad + inverse * flow
        if layer > 0:
            cot_low = gather_rows(own_grad.astype(low))

        db_qkv = (db_qkv.reshape(3, 1, local_qk) * mine[None, :, None]).reshape(-1)
        db_up = (db_up.reshape(F, 1, hidden) * mine[None, :, None]).reshape(-1)
        db = jnp.concatenate([db_qkv, db_rest, db_rest, db_up]).reshape(F * C, own_bias)
        dg = dg.reshape(2, F * C, depth).transpose(1, 0, 2).reshape(F * C, 2 * depth)
        ds = ds.reshape(2, F * C, depth).transpose(1, 0, 2).reshape(F * C, 2 * depth)
        small = jnp.concatenate(
            [db, dg, ds, jnp.zeros((F * C, small_pad - own_small), wide)], axis=1
        )
        small = small.astype(low).reshape(F, -1, LANES)
        extra = -small.shape[1] % 16
        small = jnp.pad(small, ((0, 0), (0, extra), (0, 0)))
        if aligned:
            size = (column_slabs * C * depth) + width // LANES * (hidden + out_rows)
            (payload,) = call(
                pack_kernel,
                [((F, size + small.shape[1], LANES), low)],
                [],
                d_qkv,
                d_up,
                d_down,
                d_out,
                small,
            )
        else:
            payload = jnp.concatenate(
                slabs(d_qkv.reshape(F, C * depth, 3 * local_qk))
                + slabs(d_up.reshape(F, C * depth, local_ff))
                + slabs(d_down.reshape(F, hidden, width))
                + slabs(d_out.reshape(F, out_rows, width))
                + [small],
                axis=1,
            )
        parts = lax.all_to_all(payload, "fsdp", 0, 0, tiled=False)
        pieces[layer] = jnp.sum(parts.astype(wide), axis=0)
        pieces[layer] = pieces[layer][: pieces[layer].shape[0] - extra]
    grad_tokens = own_grad.reshape(micros, 1, rows, width)

    merged = jnp.stack(pieces)
    n_cols = column_slabs * C * depth
    n_down = width // LANES * hidden
    n_out = width // LANES * out_rows
    cols = merged[:, :n_cols].reshape(layers, column_slabs, C, depth, LANES)
    cols = cols.transpose(2, 0, 1, 3, 4).reshape(C, layers, -1, LANES)
    small = merged[:, n_cols + n_down + n_out :].reshape(layers, C, -1, LANES).transpose(1, 0, 2, 3)
    home = lax.all_to_all(jnp.concatenate([cols, small], axis=2), "ctx", 0, 0, tiled=False)
    down_sum = merged[:, n_cols : n_cols + n_down].reshape(layers, -1, hidden, LANES)
    grad_down = down_sum.transpose(0, 2, 1, 3).reshape(layers, hidden, width)
    out_sum = merged[:, n_cols + n_down : n_cols + n_down + n_out]
    out_sum = out_sum.reshape(layers, -1, out_rows, LANES).transpose(0, 2, 1, 3)
    grad_out = lax.ppermute(out_sum.reshape(layers, out_rows, width), ("fsdp", "ctx"), back)

    n_own = column_slabs * depth
    columns = home[:, :, :n_own].reshape(C, layers, column_slabs, depth, LANES)
    grad_qkv = columns[:, :, :3].transpose(1, 3, 2, 0, 4).reshape(layers, depth, 3 * width)
    grad_up = columns[:, :, 3:].transpose(0, 1, 3, 2, 4).reshape(C, layers, depth, F, hidden)
    grad_up = grad_up.transpose(1, 2, 3, 0, 4).reshape(layers, depth, F * C * hidden)
    small = jnp.sum(home[:, :, n_own:], axis=0).reshape(layers, small_pad)
    grad_bias = small[:, :own_bias]
    grad_gain = small[:, own_bias : own_bias + 2 * depth].reshape(layers, 2, depth)
    grad_shift = small[:, own_bias + 2 * depth : own_small].reshape(layers, 2, depth)
    return (
        block_out,
        grad_tokens,
        grad_qkv,
        grad_out,
        grad_up,
        grad_down,
        grad_gain,
        grad_shift,
        grad_bias,
    )


def solution(mesh):
    weight = P(None, ("fsdp", "ctx"), None)
    rows = P(None, "fsdp", "ctx", None)
    feature = P(None, None, ("fsdp", "ctx"))
    flat = P(None, ("fsdp", "ctx"))
    return jax.shard_map(
        body,
        mesh=mesh,
        in_specs=(
            rows,
            rows,
            P(None, "fsdp", None),
            weight,
            weight,
            weight,
            weight,
            feature,
            feature,
            flat,
        ),
        out_specs=(rows, rows, weight, weight, weight, weight, feature, feature, flat),
        check_vma=False,
    )
```

time: 486 us -> 322 us (0.66)
  local copies, waits for them, and re-layouts: 156 us -> 57.9 us
  matrix products: 50.1 us -> 0 us
  other arithmetic: 60.6 us -> 19.6 us
  blocking collectives: 8.45 us -> 33.2 us
  Pallas kernels: 0 us -> 18.8 us
  waiting for transfers between devices: 137 us -> 126 us
    all_gather x3 -> x1, waiting for transfers between devices: 59.4 us -> 0.02 us  [gather_layer(): return lax.all_gather(payload, 'fsdp', axis=0)]
    dot_general x34 -> x0, matrix products: 46.4 us -> none  [the longest x10 13.6 us: batched(): return jnp.einsum(spec, left, right, preferred_element_type=wide)]
    all_to_all x1, waiting for transfers between devices: 0.01 us -> 40.2 us  [gather_layer(): lax.all_to_all(jnp.broadcast_to(payload[None], (F, size, LANES)), 'fsdp',...]
    slice x40 -> x5, local copies, waits for them, and re-layouts: 27.1 us -> 0.36 us  [the longest x1 0.33 us: gather_layer(): part = arrived[:, layer]]
    reshape x30 -> x4, local copies, waits for them, and re-layouts: 23 us -> 0.35 us  [the longest x2 0.17 us: layer_weights(): shifts = shifts.transpose(1, 0, 2).reshape(2, width)]
    another operation x23 -> x7, local copies, waits for them, and re-layouts: 22.7 us -> 0.23 us  [the longest x4 0.17 us: layer_weights(): return (qkv, out, up, down, gains, shifts, b_qkv[None], b_up[None], b_rest)]
    pallas_call x0 -> x8, Pallas kernels: none -> 18.8 us  [call(): pl.pallas_call(kernel, out_shape=[jax.ShapeDtypeStruct(shape, kind) for s...]
    all_gather x0 -> x2, blocking collectives: none -> 18.4 us  [the longest x1 10.9 us: body(): cot_all = lax.all_gather(cot_rows, 'ctx', axis=0).reshape(total_rows, width)]
  transfers between devices with their start and end apart: 14 -> 12, of which waited for: 8 -> 6; matrix products, arithmetic and copies ran while one was open for 28% -> 8% of each run, Pallas kernels for 0% -> 4%
where the time goes in v2:
time: 322 us; the launch traced here: 320 us
  waiting for transfers between devices  126 us (39%)
  local copies, waits for them, and re-layouts  57.9 us (18%)
  starting transfers between devices  49.3 us (15%)
  blocking collectives  33.2 us (10%)
  other arithmetic  19.6 us (6%)
  Pallas kernels  18.8 us (6%)
  between operations  15 us (5%)
    all_to_all x2, waiting for transfers between devices, body(): parts = lax.all_to_all(payload, 'fsdp', 0, 0, tiled=False)  69.6 us
    all_to_all x1, waiting for transfers between devices, gather_layer(): lax.all_to_all(jnp.broadcast_to(payload[None], (F, size, LANES)), 'fsdp',...  40.2 us
    unnamed x158, local copies, waits for them, and re-layouts  35.9 us
    all_to_all x4, starting transfers between devices, sum_rows(): parts = lax.all_to_all(parts, 'ctx', 0, 0, tiled=False)  21 us
    pallas_call x8, Pallas kernels, call(): pl.pallas_call(kernel, out_shape=[jax.ShapeDtypeStruct(shape, kind) for s...  18.8 us
    all_gather x2, blocking collectives, gather_rows(): return lax.all_gather(own, 'ctx', axis=0).reshape(total_rows, width)  14.8 us
    all_gather x1, blocking collectives, body(): cot_all = lax.all_gather(cot_rows, 'ctx', axis=0).reshape(total_rows, width)  10.9 us
    all_to_all x4, waiting for transfers between devices, sum_rows(): parts = lax.all_to_all(parts, 'ctx', 0, 0, tiled=False)  9.46 us
  transfers between devices with their start and end apart: 12, of which 6 were waited for; matrix products, arithmetic and copies ran while one was open for 8% of the time, Pallas kernels for 4%

profile of v2, /device:TPU:6, one launch (start us, length us, event | category | flops | bytes accessed | tf_op | source)
XLA Modules:
  0.0 320.3 jit_solution(11651244981703779172)
XLA Ops:
  9.5 1.2 reshape.1057
  11.9 3.9 %all-to-all-start = ((bf16[4,2,114,128]{3,1,2,0:T(2,128)(2,1)}), bf16[4,2,114,128]{3,1,2,0:T(2,128)(2,1)S(1)}, u32[]{:S(2)}, u32[]{:S(2)}) async-start(bf16[4,2,114,128]{3,1,2,0:T(2,128)(2,1)} %copy.152), calls=%async_computation | async-start | bytes 466944 | tf_op jit(solution)/shard_map/all_to_all | solution.py:310
  15.8 4.9 %collective-permute-start = (bf16[2,16,512]{2,1,0:T(8,128)(2,1)S(1)}, bf16[2,16,512]{2,1,0:T(8,128)(2,1)S(1)}, u32[]{:S(2)}, u32[]{:S(2)}) collective-permute-start(bf16[2,16,512]{2,1,0:T(8,128)(2,1)S(1)} %copy-done.68), channel_id=1, source_target_pairs={{0,0},{1,4},{2,8},{3,12},{4,16},{5,20},{6,24},{7,28},{8,1},{9,5},{... | collective-permute-start | bytes 98312 | tf_op jit(solution)/shard_map/ppermute | solution.py:311
  20.9 7.6 %all_gather.20 = bf16[4,128,512]{2,1,0:T(8,128)(2,1)} all-gather(bf16[1,128,512]{2,1,0:T(8,128)(2,1)S(1)} %bitcast.130), channel_id=1, replica_groups=mesh['fsdp'=8,'ctx'=4] {'ctx'}, dimensions={0}, use_global_device_ids=true | all-gather | bytes 655360 | tf_op jit(solution)/shard_map/all_gather | solution.py:319
  30.4 1.4 broadcast_in_dim.32
  31.8 3.8 %all-to-all-start.1 = ((bf16[8,776,128]{2,1,0:T(8,128)(2,1)}), bf16[8,776,128]{2,1,0:T(8,128)(2,1)S(1)}, u32[]{:S(2)}, u32[]{:S(2)}) async-start(bf16[8,776,128]{2,1,0:T(8,128)(2,1)} %broadcast_in_dim.32), calls=%async_computation.1 | async-start | bytes 3178496 | tf_op jit(solution)/shard_map/all_to_all | solution.py:334
  38.3 1.2 bitcast_convert_fusion.x_ref
  39.4 40.2 %all-to-all-done.1.gathered_ref = bf16[8,776,128]{2,1,0:T(8,128)(2,1)S(1)} async-done(((bf16[8,776,128]{2,1,0:T(8,128)(2,1)}), bf16[8,776,128]{2,1,0:T(8,128)(2,1)S(1)}, u32[]{:S(2)}, u32[]{:S(2)}) %all-to-all-start.1) | async-done | bytes 1589280 | tf_op jit(solution)/shard_map/all_to_all | solution.py:334
  84.1 3.4 %shard_map.170 = (bf16[512,512]{1,0:T(8,128)(2,1)}, bf16[512,512]{1,0:T(8,128)(2,1)S(1)}, bf16[512,512]{1,0:T(8,128)(2,1)S(1)}, bf16[512,384]{1,0:T(8,128)(2,1)S...) custom-call(f32[512,512]{1,0:T(8,128)S(1)} %bitcast_convert_fusion.x, ...), custom_call_target="tpu_custom_call" | custom-call | flops 3000000000 | bytes 10000000 | tf_op jit(solution)/shard_map/pallas_call | solution.py:246
  93.3 5.3 %all-to-all-start.2 = ((bf16[4,128,512]{2,1,0:T(8,128)(2,1)}), bf16[4,128,512]{2,1,0:T(8,128)(2,1)S(1)}, u32[]{:S(2)}, u32[]{:S(2)}) async-start(bf16[4,128,512]{2,1,0:T(8,128)(2,1)} %bitcast.16), calls=%async_computation.2 | async-start | bytes 1048576 | tf_op jit(solution)/shard_map/all_to_all | solution.py:393
  98.6 10.9 %all_gather.24 = bf16[4,128,512]{2,1,0:T(8,128)(2,1)S(1)} all-gather(bf16[1,128,512]{2,1,0:T(8,128)(2,1)} %bitcast.134), channel_id=1, replica_groups=mesh['fsdp'=8,'ctx'=4] {'ctx'}, dimensions={0}, use_global_device_ids=true | all-gather | bytes 655360 | tf_op jit(solution)/shard_map/all_gather | solution.py:321
  110.4 7.5 %all_gather.23 = bf16[4,128,512]{2,1,0:T(8,128)(2,1)S(1)} all-gather(bf16[1,128,512]{2,1,0:T(8,128)(2,1)S(1)} %fusion.18), channel_id=1, replica_groups=mesh['fsdp'=8,'ctx'=4] {'ctx'}, dimensions={0}, use_global_device_ids=true | all-gather | bytes 655360 | tf_op jit(solution)/shard_map/all_gather | solution.py:397
  117.9 1.2 convert_add_fusion.x_ref
  119.2 1.4 copy-done.3
  127.3 1.0 copy-done.1
  128.4 1.0 copy-done.27
  129.4 1.0 copy-done.29
  132.4 3.3 %shard_map.172 = (bf16[512,512]{1,0:T(8,128)(2,1)}, bf16[512,512]{1,0:T(8,128)(2,1)S(1)}, bf16[512,512]{1,0:T(8,128)(2,1)S(1)}, bf16[512,384]{1,0:T(8,128)(2,1)S...) custom-call(f32[512,512]{1,0:T(8,128)S(1)} %convert_add_fusion.x_ref, ...), custom_call_target="tpu_custom_call" | custom-call | flops 3000000000 | bytes 10000000 | tf_op jit(solution)/shard_map/pallas_call | solution.py:246
  135.6 4.0 %shard_map.173 = (bf16[512,512]{1,0:T(8,128)(2,1)S(1)}, bf16[512,384]{1,0:T(8,128)(2,1)S(1)}, bf16[128,512]{1,0:T(8,128)(2,1)S(1)}, bf16[512,512]{1,0:T(8,128)(2...) custom-call(bf16[512,512]{1,0:T(8,128)(2,1)S(1)} %bitcast.124, ...), custom_call_target="tpu_custom_call" | custom-call | flops 3000000000 | bytes 10000000 | tf_op jit(solution)/shard_map/pallas_call | solution.py:246
  143.5 5.2 %all-to-all-start.4 = ((bf16[4,128,512]{2,1,0:T(8,128)(2,1)}), bf16[4,128,512]{2,1,0:T(8,128)(2,1)S(1)}, u32[]{:S(2)}, u32[]{:S(2)}) async-start(bf16[4,128,512]{2,1,0:T(8,128)(2,1)} %bitcast.126), calls=%async_computation.4 | async-start | bytes 1048576 | tf_op jit(solution)/shard_map/all_to_all | solution.py:393
  148.7 1.1 convert_reduce_fusion.8
  152.1 3.8 %all-to-all-done.4 = bf16[4,128,512]{2,1,0:T(8,128)(2,1)S(1)} async-done(((bf16[4,128,512]{2,1,0:T(8,128)(2,1)}), bf16[4,128,512]{2,1,0:T(8,128)(2,1)S(1)}, u32[]{:S(2)}, u32[]{:S(2)}) %all-to-all-start.4) | async-done | bytes 524320 | tf_op jit(solution)/shard_map/all_to_all | solution.py:393
  156.7 5.8 %all-to-all-start.3 = ((bf16[4,128,512]{2,1,0:T(8,128)(2,1)}), bf16[4,128,512]{2,1,0:T(8,128)(2,1)}, u32[]{:S(2)}, u32[]{:S(2)}) async-start(bf16[4,128,512]{2,1,0:T(8,128)(2,1)} %bitcast.31), calls=%async_computation.3 | async-start | bytes 1048576 | tf_op jit(solution)/shard_map/all_to_all | solution.py:393
  162.5 1.4 convert_reduce_fusion.4
  164.5 1.2 fusion.11
  165.8 1.3 fusion.17
  167.1 7.3 %all_gather.25 = bf16[4,128,512]{2,1,0:T(8,128)(2,1)S(1)} all-gather(bf16[1,128,512]{2,1,0:T(8,128)(2,1)S(1)} %fusion.17), channel_id=1, replica_groups=mesh['fsdp'=8,'ctx'=4] {'ctx'}, dimensions={0}, use_global_device_ids=true | all-gather | bytes 655360 | tf_op jit(solution)/shard_map/all_gather | solution.py:397
  174.5 1.2 copy-done.7
  175.7 1.0 copy-done.15
  176.7 1.0 copy-done.17
  177.8 1.0 copy-done.19
  183.7 4.7 %shard_map.174 = (bf16[512,512]{1,0:T(8,128)(2,1)}, bf16[512,384]{1,0:T(8,128)(2,1)S(1)}, bf16[128,512]{1,0:T(8,128)(2,1)S(1)}, bf16[512,512]{1,0:T(8,128)(2,1)S...) custom-call(bf16[512,512]{1,0:T(8,128)(2,1)S(1)} %bitcast.125, ...), custom_call_target="tpu_custom_call" | custom-call | flops 3000000000 | bytes 10000000 | tf_op jit(solution)/shard_map/pallas_call | solution.py:246
  192.6 1.4 fusion.34
  194.9 4.7 %all-to-all-start.5 = ((bf16[4,128,512]{2,1,0:T(8,128)(2,1)}), bf16[4,128,512]{2,1,0:T(8,128)(2,1)}, u32[]{:S(2)}, u32[]{:S(2)}) async-start(bf16[4,128,512]{2,1,0:T(8,128)(2,1)} %bitcast.41), calls=%async_computation.5 | async-start | bytes 1048576 | tf_op jit(solution)/shard_map/all_to_all | solution.py:393
  199.8 1.5 shard_map.175
  201.3 5.7 %all-to-all-done.5 = bf16[4,128,512]{2,1,0:T(8,128)(2,1)} async-done(((bf16[4,128,512]{2,1,0:T(8,128)(2,1)}), bf16[4,128,512]{2,1,0:T(8,128)(2,1)}, u32[]{:S(2)}, u32[]{:S(2)}) %all-to-all-start.5) | async-done | bytes 524320 | tf_op jit(solution)/shard_map/all_to_all | solution.py:393
  206.9 4.2 %all-to-all-start.6 = ((bf16[8,784,128]{2,1,0:T(8,128)(2,1)}), bf16[8,784,128]{2,1,0:T(8,128)(2,1)S(1)}, u32[]{:S(2)}, u32[]{:S(2)}) async-start(bf16[8,784,128]{2,1,0:T(8,128)(2,1)} %shard_map.175), calls=%async_computation.6 | async-start | bytes 3211264 | tf_op jit(solution)/shard_map/all_to_all | solution.py:529
  211.2 1.5 shard_map.176
  212.7 35.8 %all-to-all-done.6 = bf16[8,784,128]{2,1,0:T(8,128)(2,1)S(1)} async-done(((bf16[8,784,128]{2,1,0:T(8,128)(2,1)}), bf16[8,784,128]{2,1,0:T(8,128)(2,1)S(1)}, u32[]{:S(2)}, u32[]{:S(2)}) %all-to-all-start.6) | async-done | bytes 1605664 | tf_op jit(solution)/shard_map/all_to_all | solution.py:529
  248.5 4.7 %all-to-all-start.7 = ((bf16[8,784,128]{2,1,0:T(8,128)(2,1)}), bf16[8,784,128]{2,1,0:T(8,128)(2,1)}, u32[]{:S(2)}, u32[]{:S(2)}) async-start(bf16[8,784,128]{2,1,0:T(8,128)(2,1)} %shard_map.176), calls=%async_computation.7 | async-start | bytes 3211264 | tf_op jit(solution)/shard_map/all_to_all | solution.py:529
  253.3 1.1 convert_reduce_fusion.6
  254.5 1.2 convert_reduce_fusion.2
  256.3 33.8 %all-to-all-done.7 = bf16[8,784,128]{2,1,0:T(8,128)(2,1)} async-done(((bf16[8,784,128]{2,1,0:T(8,128)(2,1)}), bf16[8,784,128]{2,1,0:T(8,128)(2,1)}, u32[]{:S(2)}, u32[]{:S(2)}) %all-to-all-start.7) | async-done | bytes 1605664 | tf_op jit(solution)/shard_map/all_to_all | solution.py:529
  290.1 1.7 convert_reduce_fusion
  293.0 4.8 %all-to-all-start.8 = ((f32[4,2,114,128]{3,1,2,0:T(2,128)}), f32[4,2,114,128]{3,1,2,0:T(2,128)S(1)}, u32[]{:S(2)}, u32[]{:S(2)}) async-start(f32[4,2,114,128]{3,1,2,0:T(2,128)} %copy.173), calls=%async_computation.8 | async-start | bytes 933888 | tf_op jit(solution)/shard_map/all_to_all | solution.py:541
  298.8 1.9 collective-permute-start.1
  301.5 7.1 %collective-permute-done.1 = f32[2,16,512]{2,1,0:T(8,128)S(1)} collective-permute-done((f32[2,16,512]{2,1,0:T(8,128)S(1)}, f32[2,16,512]{2,1,0:T(8,128)S(1)}, u32[]{:S(2)}, u32[]{:S(2)}) %collective-permute-start.1) | collective-permute-done | bytes 65568 | tf_op jit(solution)/shard_map/ppermute | solution.py:546
  310.2 1.1 reshape.1103
  (315 shorter events, 52.7 us)
Async XLA Ops:
  7.2 3.8 %copy-start.64 = (bf16[2,16,1536]{2,1,0:T(8,128)(2,1)S(1)}, bf16[2,16,1536]{2,1,0:T(8,128)(2,1)}, u32[]{:S(2)}) copy-start(bf16[2,16,1536]{2,1,0:T(8,128)(2,1)} %param.13) | copy-start | bytes 294916
  9.5 6.3 %copy-start.68 = (bf16[2,16,512]{2,1,0:T(8,128)(2,1)S(1)}, bf16[2,16,512]{2,1,0:T(8,128)(2,1)}, u32[]{:S(2)}) copy-start(bf16[2,16,512]{2,1,0:T(8,128)(2,1)} %param.14) | copy-start | bytes 98308
  10.7 10.1 %copy-start.63 = (bf16[2,64,512]{2,1,0:T(8,128)(2,1)S(1)}, bf16[2,64,512]{2,1,0:T(8,128)(2,1)}, u32[]{:S(2)}) copy-start(bf16[2,64,512]{2,1,0:T(8,128)(2,1)} %param.16) | copy-start | bytes 393220
  10.7 10.2 %copy-start.52 = (bf16[2,1,64,512]{3,2,1,0:T(8,128)(2,1)S(1)}, bf16[2,1,64,512]{3,2,1,0:T(8,128)(2,1)}, u32[]{:S(2)}) copy-start(bf16[2,1,64,512]{3,2,1,0:T(8,128)(2,1)} %param.10) | copy-start | bytes 393220
  10.9 17.5 %copy-start.66 = (s32[2,1,5]{2,1,0:T(1,128)S(1)}, s32[2,1,5]{2,1,0:T(1,128)}, u32[]{:S(2)}) copy-start(s32[2,1,5]{2,1,0:T(1,128)} %param.12) | copy-start | bytes 124
  11.9 17.9 %all-to-all-start = ((bf16[4,2,114,128]{3,1,2,0:T(2,128)(2,1)}), bf16[4,2,114,128]{3,1,2,0:T(2,128)(2,1)S(1)}, u32[]{:S(2)}, u32[]{:S(2)}) async-start(bf16[4,2,114,128]{3,1,2,0:T(2,128)(2,1)} %copy.152), calls=%async_computation | async-start | bytes 466944 | tf_op jit(solution)/shard_map/all_to_all | solution.py:310
  15.8 14.0 %collective-permute-start = (bf16[2,16,512]{2,1,0:T(8,128)(2,1)S(1)}, bf16[2,16,512]{2,1,0:T(8,128)(2,1)S(1)}, u32[]{:S(2)}, u32[]{:S(2)}) collective-permute-start(bf16[2,16,512]{2,1,0:T(8,128)(2,1)S(1)} %copy-done.68), channel_id=1, source_target_pairs={{0,0},{1,4},{2,8},{3,12},{4,16},{5,20},{6,24},{7,28},{8,1},{9,5},{... | collective-permute-start | bytes 98312 | tf_op jit(solution)/shard_map/ppermute | solution.py:311
  31.8 47.8 %all-to-all-start.1 = ((bf16[8,776,128]{2,1,0:T(8,128)(2,1)}), bf16[8,776,128]{2,1,0:T(8,128)(2,1)S(1)}, u32[]{:S(2)}, u32[]{:S(2)}) async-start(bf16[8,776,128]{2,1,0:T(8,128)(2,1)} %broadcast_in_dim.32), calls=%async_computation.1 | async-start | bytes 3178496 | tf_op jit(solution)/shard_map/all_to_all | solution.py:334
  35.6 83.6 %all-gather.3.cloned.1.call-start = ((), (), s32[]{:S(2)}) async-start(), calls=%async_computation.9 | async-start | bytes 1787904 | tf_op jit(solution)/shard_map/all_gather | solution.py:337
  83.1 1.0 copy-start
  83.4 4.1 %copy-start.12 = (bf16[512,512]{1,0:T(8,128)(2,1)}, bf16[512,512]{1,0:T(8,128)(2,1)S(1)}, u32[]{:S(2)}) copy-start(bf16[512,512]{1,0:T(8,128)(2,1)S(1)} %get-tuple-element.55.up_ref) | copy-start | bytes 1572868
  83.4 4.1 %copy-start.14 = (bf16[512,512]{1,0:T(8,128)(2,1)}, bf16[512,512]{1,0:T(8,128)(2,1)S(1)}, u32[]{:S(2)}) copy-start(bf16[512,512]{1,0:T(8,128)(2,1)S(1)} %get-tuple-element.56.down_ref) | copy-start | bytes 1572868
  83.4 4.1 %copy-start.32 = (bf16[512,384]{1,0:T(8,128)(2,1)}, bf16[512,384]{1,0:T(8,128)(2,1)S(1)}, u32[]{:S(2)}) copy-start(bf16[512,384]{1,0:T(8,128)(2,1)S(1)} %get-tuple-element.53.qkv_ref) | copy-start | bytes 1179652
  83.4 4.1 %copy-start.43 = (bf16[128,512]{1,0:T(8,128)(2,1)}, bf16[128,512]{1,0:T(8,128)(2,1)S(1)}, u32[]{:S(2)}) copy-start(bf16[128,512]{1,0:T(8,128)(2,1)S(1)} %get-tuple-element.54.out_ref) | copy-start | bytes 393220
  93.3 16.3 %all-to-all-start.2 = ((bf16[4,128,512]{2,1,0:T(8,128)(2,1)}), bf16[4,128,512]{2,1,0:T(8,128)(2,1)S(1)}, u32[]{:S(2)}, u32[]{:S(2)}) async-start(bf16[4,128,512]{2,1,0:T(8,128)(2,1)} %bitcast.16), calls=%async_computation.2 | async-start | bytes 1048576 | tf_op jit(solution)/shard_map/all_to_all | solution.py:393
  119.2 1.4 copy-start.3
  127.3 1.0 copy-start.1
  129.4 1.0 copy-start.29
  132.4 3.3 %copy-start.40 = (bf16[512,384]{1,0:T(8,128)(2,1)S(1)}, bf16[512,384]{1,0:T(8,128)(2,1)}, u32[]{:S(2)}) copy-start(bf16[512,384]{1,0:T(8,128)(2,1)} %copy-done.38) | copy-start | bytes 1179652
  132.4 3.3 %copy-start.51 = (bf16[128,512]{1,0:T(8,128)(2,1)S(1)}, bf16[128,512]{1,0:T(8,128)(2,1)}, u32[]{:S(2)}) copy-start(bf16[128,512]{1,0:T(8,128)(2,1)} %copy-done.49) | copy-start | bytes 393220
  143.5 6.4 %copy-start.53 = (bf16[2,1,64,512]{3,2,1,0:T(8,128)(2,1)S(1)}, bf16[2,1,64,512]{3,2,1,0:T(8,128)(2,1)}, u32[]{:S(2)}) copy-start(bf16[2,1,64,512]{3,2,1,0:T(8,128)(2,1)} %param.10) | copy-start | bytes 393220
  143.5 12.4 %all-to-all-start.4 = ((bf16[4,128,512]{2,1,0:T(8,128)(2,1)}), bf16[4,128,512]{2,1,0:T(8,128)(2,1)S(1)}, u32[]{:S(2)}, u32[]{:S(2)}) async-start(bf16[4,128,512]{2,1,0:T(8,128)(2,1)} %bitcast.126), calls=%async_computation.4 | async-start | bytes 1048576 | tf_op jit(solution)/shard_map/all_to_all | solution.py:393
  149.8 6.0 %copy-start.58 = (bf16[2,1,64,512]{3,2,1,0:T(8,128)(2,1)}, bf16[2,1,64,512]{3,2,1,0:T(8,128)(2,1)S(1)}, u32[]{:S(2)}) copy-start(bf16[2,1,64,512]{3,2,1,0:T(8,128)(2,1)S(1)} %get-tuple-element.107) | copy-start | bytes 393220
  156.7 38.2 %all-to-all-start.3 = ((bf16[4,128,512]{2,1,0:T(8,128)(2,1)}), bf16[4,128,512]{2,1,0:T(8,128)(2,1)}, u32[]{:S(2)}, u32[]{:S(2)}) async-start(bf16[4,128,512]{2,1,0:T(8,128)(2,1)} %bitcast.31), calls=%async_computation.3 | async-start | bytes 1048576 | tf_op jit(solution)/shard_map/all_to_all | solution.py:393
  162.4 12.0 %copy-start.5 = (f32[4,256,256]{2,1,0:T(8,128)S(1)}, f32[4,256,256]{2,1,0:T(8,128)}, u32[]{:S(2)}) copy-start(f32[4,256,256]{2,1,0:T(8,128)} %copy-done.4) | copy-start | bytes 3145732
  162.5 12.0 %copy-start.13 = (bf16[512,512]{1,0:T(8,128)(2,1)S(1)}, bf16[512,512]{1,0:T(8,128)(2,1)}, u32[]{:S(2)}) copy-start(bf16[512,512]{1,0:T(8,128)(2,1)} %copy-done.12) | copy-start | bytes 1572868
  174.5 1.2 copy-start.7
  175.7 1.0 copy-start.15
  176.7 1.0 copy-start.17
  191.4 8.3 %copy-start.67 = (bf16[256]{0:T(256)(128)(2,1)S(1)}, bf16[256]{0:T(256)(128)(2,1)}, u32[]{:S(2)}) copy-start(bf16[256]{0:T(256)(128)(2,1)} %pad.29.clone) | copy-start | bytes 1540
  191.4 8.4 %copy-start.23 = (bf16[512,512]{1,0:T(8,128)(2,1)S(1)}, bf16[512,512]{1,0:T(8,128)(2,1)}, u32[]{:S(2)}) copy-start(bf16[512,512]{1,0:T(8,128)(2,1)} %copy-done.22) | copy-start | bytes 1572868
  191.4 8.4 %copy-start.25 = (bf16[512,512]{1,0:T(8,128)(2,1)S(1)}, bf16[512,512]{1,0:T(8,128)(2,1)}, u32[]{:S(2)}) copy-start(bf16[512,512]{1,0:T(8,128)(2,1)} %copy-done.24) | copy-start | bytes 1572868
  191.4 8.4 %copy-start.37 = (bf16[512,384]{1,0:T(8,128)(2,1)S(1)}, bf16[512,384]{1,0:T(8,128)(2,1)}, u32[]{:S(2)}) copy-start(bf16[512,384]{1,0:T(8,128)(2,1)} %copy-done.36) | copy-start | bytes 1179652
  191.4 8.4 %copy-start.48 = (bf16[128,512]{1,0:T(8,128)(2,1)S(1)}, bf16[128,512]{1,0:T(8,128)(2,1)}, u32[]{:S(2)}) copy-start(bf16[128,512]{1,0:T(8,128)(2,1)} %copy-done.47) | copy-start | bytes 393220
  194.9 12.0 %all-to-all-start.5 = ((bf16[4,128,512]{2,1,0:T(8,128)(2,1)}), bf16[4,128,512]{2,1,0:T(8,128)(2,1)}, u32[]{:S(2)}, u32[]{:S(2)}) async-start(bf16[4,128,512]{2,1,0:T(8,128)(2,1)} %bitcast.41), calls=%async_computation.5 | async-start | bytes 1048576 | tf_op jit(solution)/shard_map/all_to_all | solution.py:393
  201.3 9.9 %copy-start.9 = (bf16[512,512]{1,0:T(8,128)(2,1)S(1)}, bf16[512,512]{1,0:T(8,128)(2,1)}, u32[]{:S(2)}) copy-start(bf16[512,512]{1,0:T(8,128)(2,1)} %copy-done.8) | copy-start | bytes 1572868
  201.3 9.9 %copy-start.11 = (bf16[512,512]{1,0:T(8,128)(2,1)S(1)}, bf16[512,512]{1,0:T(8,128)(2,1)}, u32[]{:S(2)}) copy-start(bf16[512,512]{1,0:T(8,128)(2,1)} %copy-done.10) | copy-start | bytes 1572868
  201.3 9.9 %copy-start.31 = (bf16[512,384]{1,0:T(8,128)(2,1)S(1)}, bf16[512,384]{1,0:T(8,128)(2,1)}, u32[]{:S(2)}) copy-start(bf16[512,384]{1,0:T(8,128)(2,1)} %copy-done.30) | copy-start | bytes 1179652
  201.3 9.9 %copy-start.42 = (bf16[128,512]{1,0:T(8,128)(2,1)S(1)}, bf16[128,512]{1,0:T(8,128)(2,1)}, u32[]{:S(2)}) copy-start(bf16[128,512]{1,0:T(8,128)(2,1)} %copy-done.41) | copy-start | bytes 393220
  206.9 41.6 %all-to-all-start.6 = ((bf16[8,784,128]{2,1,0:T(8,128)(2,1)}), bf16[8,784,128]{2,1,0:T(8,128)(2,1)S(1)}, u32[]{:S(2)}, u32[]{:S(2)}) async-start(bf16[8,784,128]{2,1,0:T(8,128)(2,1)} %shard_map.175), calls=%async_computation.6 | async-start | bytes 3211264 | tf_op jit(solution)/shard_map/all_to_all | solution.py:529
  248.5 41.6 %all-to-all-start.7 = ((bf16[8,784,128]{2,1,0:T(8,128)(2,1)}), bf16[8,784,128]{2,1,0:T(8,128)(2,1)}, u32[]{:S(2)}, u32[]{:S(2)}) async-start(bf16[8,784,128]{2,1,0:T(8,128)(2,1)} %shard_map.176), calls=%async_computation.7 | async-start | bytes 3211264 | tf_op jit(solution)/shard_map/all_to_all | solution.py:529
  253.2 2.6 copy-start.54
  291.9 5.9 %copy-start.56 = (f32[128,512]{1,0:T(8,128)S(1)}, f32[128,512]{1,0:T(8,128)}, u32[]{:S(2)}) copy-start(f32[128,512]{1,0:T(8,128)} %copy-done.55) | copy-start | bytes 786436
  291.9 5.9 %copy-start.59 = (bf16[2,1,64,512]{3,2,1,0:T(8,128)(2,1)S(1)}, bf16[2,1,64,512]{3,2,1,0:T(8,128)(2,1)}, u32[]{:S(2)}) copy-start(bf16[2,1,64,512]{3,2,1,0:T(8,128)(2,1)} %copy-done.58) | copy-start | bytes 393220
  291.9 5.9 %copy-start.60 = (bf16[2,1,64,512]{3,2,1,0:T(8,128)(2,1)S(1)}, bf16[2,1,64,512]{3,2,1,0:T(8,128)(2,1)}, u32[]{:S(2)}) copy-start(bf16[2,1,64,512]{3,2,1,0:T(8,128)(2,1)} %param.11) | copy-start | bytes 393220
  293.0 15.6 %all-to-all-start.8 = ((f32[4,2,114,128]{3,1,2,0:T(2,128)}), f32[4,2,114,128]{3,1,2,0:T(2,128)S(1)}, u32[]{:S(2)}, u32[]{:S(2)}) async-start(f32[4,2,114,128]{3,1,2,0:T(2,128)} %copy.173), calls=%async_computation.8 | async-start | bytes 933888 | tf_op jit(solution)/shard_map/all_to_all | solution.py:541
  298.8 9.8 %collective-permute-start.1 = (f32[2,16,512]{2,1,0:T(8,128)S(1)}, f32[2,16,512]{2,1,0:T(8,128)S(1)}, u32[]{:S(2)}, u32[]{:S(2)}) collective-permute-start(f32[2,16,512]{2,1,0:T(8,128)S(1)} %bitcast.166), channel_id=1, source_target_pairs={{0,0},{4,1},{8,2},{12,3},{16,4},{20,5},{24,6},{28,7},{1,8},{5,9},{... | collective-permute-start | bytes 196616 | tf_op jit(solution)/shard_map/ppermute | solution.py:546
  311.4 2.0 copy-start.65
  (33 other events, 27.5 us)
Sparse Core Ops, SparseCore 0:
  39.2 57.9 all-gather.2
